TPU v7x, 768 devices: a whole 4x8x12 slice. The times are simulated.
768 devices in a mesh: fsdp: 24 (over z_lo, x), tp: 32 (over z_hi, y, core).
Axes of the slice: x: 4, y: 8, z: 12 (z_hi: 2, z_lo: 6; z = z_hi * 6 + z_lo), core: 2. Of those that a mesh axis runs over, the one named last changes fastest.
Arguments:
- codes: bfloat16 [15360, 8192], P('fsdp', 'tp'), may hold values from -448 to 448, as said below
- offsets: int32 [120, 64], P('fsdp', 'tp'), may hold values from -8 to -4
- responses: bfloat16 [6144, 15360], P('fsdp'), may hold values from -6 to 6
- head: bfloat16 [8192], P('tp'), may hold values from -0.0625 to 0.0625
Outputs:
- projected_out: bfloat16 [6144, 8192], P('fsdp', 'tp')
- scores: float32 [6144], P('fsdp')
Inputs may be any that keep to these rules, and one draw needn't show every extreme that they name: `codes`: code values held in bfloat16.
All inputs are finite; a program needn't handle non-finite values.
Results may differ from a plain program's by a relative error of at most 0.0034.
Values may be sent and summed in bfloat16 or wider, within the bound.
A program may use at most 64 MiB of HBM per device.

v0:
```python
import jax
import jax.numpy as jnp
from jax import lax
from jax.sharding import PartitionSpec as P

BLK = 128
D = 8192


def block_scales(codes, offsets):
    rows, cols = codes.shape
    blocks = jnp.abs(codes.astype(jnp.float32)).reshape(rows // BLK, BLK, cols // BLK, BLK)
    amax = jnp.max(blocks, axis=(1, 3))
    return jnp.exp2(offsets.astype(jnp.float32)) / (amax + 1e-06)


def dequantize(codes, scales):
    rows, cols = codes.shape
    blocks = (
        codes.astype(jnp.float32).reshape(rows // BLK, BLK, cols // BLK, BLK)
        * scales[:, None, :, None]
    )
    return blocks.reshape(rows, cols).astype(jnp.bfloat16)


def on_device(codes, offsets, responses, head):
    scales = block_scales(codes, offsets)
    gathered = lax.all_gather(codes, "fsdp", axis=0, tiled=True)
    all_scales = lax.all_gather(scales, "fsdp", axis=0, tiled=True)
    projected = jnp.dot(
        responses, dequantize(gathered, all_scales), preferred_element_type=jnp.float32
    )
    squares = jnp.sum(projected * projected, axis=1)
    along = jnp.sum(projected * head.astype(jnp.float32)[None, :], axis=1)
    total_squares, total_along = lax.psum((squares, along), "tp")
    power = total_squares / D
    scores = total_along / jnp.sqrt(power + 1e-06)
    return (projected.astype(jnp.bfloat16), scores)


def solution(mesh):
    in_specs = (P("fsdp", "tp"), P("fsdp", "tp"), P("fsdp", None), P("tp"))
    out_specs = (P("fsdp", "tp"), P("fsdp"))
    return jax.shard_map(
        on_device, mesh=mesh, in_specs=in_specs, out_specs=out_specs, check_vma=False
    )
```

profile of v0, /device:TPU:1, one launch (start us, length us, event | category | flops | bytes accessed | tf_op | source)
XLA Modules:
  0.0 319.3 jit_solution(910117500621763858)
XLA Ops:
  7.2 0.0 all-gather.3.cloned.1.call-start
  7.2 0.7 all-gather.3.cloned.1.call-update
  7.9 0.7 convert_element_type.27
  8.6 0.8 copy.10
  9.3 1.0 convert_abs_fusion
  10.4 0.3 reshape.12
  10.7 0.3 reduce_max.9
  11.0 0.1 copy.11
  11.1 77.4 %all-gather = f32[24,5,2]{1,2,0:T(2,128)S(1)} all-gather(f32[1,5,2]{1,2,0:T(2,128)S(1)} %bitcast.16), channel_id=1, replica_groups=mesh['fsdp'=24,'tp'=32] {'fsdp'}, dimensions={0}, use_global_device_ids=true | all-gather | bytes 1000 | tf_op jit(solution)/shard_map/all_gather | solution.py:29
  88.5 0.1 reshape.14
  88.6 0.1 copy.13
  88.8 84.9 %all-gather.3.cloned.1.call-done = bf16[15360,256]{1,0:T(8,128)(2,1)} async-done(((bf16[640,256]{1,0:T(8,128)(2,1)}), bf16[15360,256]{1,0:T(8,128)(2,1)}) %all-gather.3.cloned.1.call-update) | async-done | bytes 7864336 | tf_op jit(solution)/shard_map/all_gather | solution.py:28
  173.7 6.2 %mul.24 = f32[120,128,2,128]{3,2,1,0:T(2,128)} broadcast(f32[120,2]{1,0:T(8,128)S(1)} %copy.13), dimensions={0,2} | broadcast | bytes 15729600 | tf_op jit(solution)/shard_map/mul | solution.py:20
  179.9 13.3 %multiply_reduce_fusion = (f32[256]{0:T(256)S(1)}, f32[256]{0:T(256)S(1)}, bf16[256,256]{0,1:T(8,128)(2,1)S(1)}) fusion(f32[256]{0:T(256)S(1)} %convert_element_type.27, bf16[256,15360]{1,0:T(8,128)(2,1)} %param.6, f32[1920,8,2,128]{3,2,1,0:T(2,128)} %bitcast.15, bf16[15360,256]{1,0:T(8,128)(2,1)} %all-gather.3.cloned.1.call-done), kind=kOutput, calls=%fused_computation.4 | convolution fusion | flops 2025389568 | bytes 31591424 | tf_op jit(solution)/shard_map/dot_general | solution.py:30
  193.3 0.8 copy.14
  194.0 117.9 %all-reduce = (f32[256]{0:T(256)S(1)}, f32[256]{0:T(256)S(1)}) all-reduce(f32[256]{0:T(256)S(1)} %get-tuple-element.9, f32[256]{0:T(256)S(1)} %get-tuple-element.8), channel_id=1, replica_groups=mesh['fsdp'=24,'tp'=32] {'tp'}, use_global_device_ids=true, to_apply=%region_2.0 | all-reduce | flops 512 | bytes 4096 | tf_op jit(solution)/shard_map/psum | solution.py:35
  311.9 0.6 rsqrt_multiply_fusion
  (2 shorter events, 0.0 us)
Async XLA Ops:
  7.2 166.5 %all-gather.3.cloned.1.call-start = ((), (), s32[]{:S(2)}) async-start(), calls=%async_computation | async-start | bytes 8192000 | tf_op jit(solution)/shard_map/all_gather | solution.py:28
Sparse Core Ops, SparseCore 0:
  10.4 163.2 all-gather.2
where the time goes:
time: 320 us; the launch traced here: 319 us
  blocking collectives  195 us (61%)
  waiting for transfers between devices  85.6 us (27%)
  between operations  14 us (4%)
  matrix products  13.3 us (4%)
  local copies, waits for them, and re-layouts  8.4 us (3%)
    psum x1, blocking collectives, on_device(): total_squares, total_along = lax.psum((squares, along), 'tp')  118 us
    all_gather x1, waiting for transfers between devices, on_device(): gathered = lax.all_gather(codes, 'fsdp', axis=0, tiled=True)  84.9 us
    all_gather x1, blocking collectives, on_device(): all_scales = lax.all_gather(scales, 'fsdp', axis=0, tiled=True)  77.4 us
    dot_general x1, matrix products, on_device(): jnp.dot(responses, dequantize(gathered, all_scales), preferred_element_ty...  13.3 us
  transfers between devices with their start and end apart: 1, of which 1 were waited for; matrix products, arithmetic and copies ran while one was open for 1% of the time, Pallas kernels for 0%

commit v1 on v0

v1 whole, which is shorter than its diff:
```python
import jax
import jax.numpy as jnp
from jax import lax
from jax.experimental import pallas as pl
from jax.experimental.pallas import tpu as pltpu
from jax.sharding import PartitionSpec as P

MESH = pl.DeviceIdType.MESH
BLK = 128
D = 8192
NX, NY, NZ, NH = 4, 8, 6, 3
ROWS = 256
CHUNK = 640
COLS = 256
HALF = NX * NH * CHUNK
SLOTS = NX * NH
ZF = 512
SUB = HALF // 2
PIECE = ROWS // (2 * NY)


def device(x, y, zl, zh, c):
    return (zl * NX + x, (zh * NY + y) * 2 + c)


def kernel(
    codes, offsets, responses, head, out, scores,
    rall, w, acc, pin, s0, s1, ys, z0, z1,
    own_sem, inj_s, inj_r, ring_s, ring_r, sib_s, sib_r,
    wz_s, wz_r, wx_s, wx_r, p_s, p_r, sc_s, sc_r,
):
    f, t = lax.axis_index("fsdp"), lax.axis_index("tp")
    x, zl = f % NX, f // NX
    c, y, zh = t % 2, (t // 2) % NY, t // (2 * NY)
    h, p = zl // NH, zl % NH

    sibling = device(x, y, zl, zh, 1 - c)

    def at_x(e):
        return device((x + e) % NX, y, zl, zh, c)

    def at_z(e):
        return device(x, y, h * NH + (p + e) % NH, zh, c)

    def at_y(e):
        return device(x, (y + e + NY) % NY, zl, zh, c)

    z = zh * NZ + zl
    near = jnp.where(zl < 2, z + 10, jnp.where(zl == 2, z + 1, jnp.where(zl == 3, z + 11, z + 2))) % (2 * NZ)
    wants = device(x, y, near % NZ, near // NZ, c)
    mate_zl = jnp.where(zl < 2, zl + 4, jnp.where(zl == 2, 3, jnp.where(zl == 3, 2, zl - 4)))
    mate = device(x, y, mate_zl, zh, c)
    other = device(x, y, zl, 1 - zh, c)

    barrier = pltpu.get_barrier_semaphore()
    partners = [sibling, wants, mate, other]
    partners += [at_x(e) for e in range(1, NX)]
    partners += [at_z(e) for e in range(1, NH)]
    partners += [at_y(e) for e in range(1, NY)]
    for partner in partners:
        pl.semaphore_signal(barrier, inc=1, device_id=partner, device_id_type=MESH)

    own = pltpu.make_async_copy(
        responses.at[:, pl.ds(pl.multiple_of(h * HALF, 128), HALF)],
        rall.at[pl.ds(0, ROWS)],
        own_sem,
    )
    own.start()

    def slot(xe, pe):
        return ((p + pe) % NH) * NX + (x + xe) % NX

    mine = slot(0, 0)
    for i in range(CHUNK // BLK):
        for j in range(COLS // BLK):
            block = codes[i * BLK : (i + 1) * BLK, j * BLK : (j + 1) * BLK].astype(jnp.float32)
            amax = jnp.max(jnp.max(jnp.abs(block), axis=0, keepdims=True), axis=1, keepdims=True)
            scale = jnp.exp2(offsets[i : i + 1, j : j + 1].astype(jnp.float32)) / (amax + 1e-06)
            w[mine, i * BLK : (i + 1) * BLK, j * BLK : (j + 1) * BLK] = (block * scale).astype(jnp.bfloat16)

    pl.semaphore_wait(barrier, len(partners))

    sent = []

    def send(src, dst, send_sem, recv_sem, to):
        copy = pltpu.make_async_remote_copy(
            src_ref=src, dst_ref=dst, send_sem=send_sem, recv_sem=recv_sem,
            device_id=to, device_id_type=MESH,
        )
        copy.start()
        sent.append(copy)

    def arrived(dst, send_sem, recv_sem):
        pltpu.make_async_remote_copy(
            src_ref=dst, dst_ref=dst, send_sem=send_sem, recv_sem=recv_sem,
            device_id=sibling, device_id_type=MESH,
        ).wait_recv()

    def piece(yo, core, k):
        row = pl.multiple_of(ROWS + 2 * PIECE * yo + PIECE * core, PIECE)
        return rall.at[pl.ds(row, PIECE), pl.ds(k * SUB, SUB)]

    def zpart(s):
        return w.at[s, pl.ds(0, ZF)]

    def xpart(s):
        return w.at[s, pl.ds(ZF, CHUNK - ZF)]

    count = {"wz": 0, "wx": 0, "ring": 0}

    def send_w(kind, s, to):
        n = count[kind]
        count[kind] += 1
        ref = zpart(s) if kind == "wz" else xpart(s)
        sems, recv = (wz_s, wz_r) if kind == "wz" else (wx_s, wx_r)
        send(ref, ref, sems.at[n], recv.at[s], to)

    for k in range(2):
        row = pl.multiple_of(2 * PIECE * y + PIECE * c, PIECE)
        col = pl.multiple_of((1 - h) * HALF + k * SUB, 128)
        send(
            responses.at[pl.ds(row, PIECE), pl.ds(col, SUB)],
            piece(y, c, k), inj_s.at[k], inj_r.at[k], wants,
        )
    for e in range(1, NX):
        send_w("wx", mine, at_x(e))
    for e in range(1, NH):
        send_w("wz", mine, at_z(e))
    for e in range(1, NX):
        send_w("wz", mine, at_x(e))
    for e in range(1, NH):
        send_w("wx", mine, at_z(e))

    def ring(dir_, k, d):
        yo = (y - dir_ * d + NY) % NY
        ref = piece(yo, c, k)
        last = 4 if (dir_ == 1) == (k == 0) else 3
        i = (0 if dir_ == 1 else 1) * 8 + k * 4
        if d > 0:
            arrived(ref, ring_s.at[i + d - 1], ring_r.at[i + d - 1])
        if d < last:
            send(ref, ref, ring_s.at[i + d], ring_r.at[i + d], at_y(dir_))
        if d > 0 or dir_ == 1:
            n = count["ring"]
            count["ring"] += 1
            send(ref, ref, sib_s.at[n], sib_r.at[n], sibling)
            sibs.append((yo, k, n))

    sibs = []

    def ring_step(d):
        for k in range(2):
            for dir_ in (1, -1):
                if d <= (4 if (dir_ == 1) == (k == 0) else 3):
                    ring(dir_, k, d)

    def forward_x(xe):
        s = slot(xe, 0)
        arrived(xpart(s), wx_s.at[0], wx_r.at[s])
        for e in range(1, NH):
            send_w("wx", s, at_z(e))

    def forward_z(pe):
        s = slot(0, pe)
        arrived(zpart(s), wz_s.at[0], wz_r.at[s])
        for e in range(1, NX):
            send_w("wz", s, at_x(e))

    for k in range(2):
        arrived(piece(y, c, k), inj_s.at[k], inj_r.at[k])
        ring(1, k, 0)
        ring(-1, k, 0)
    for xe in (1, 3, 2):
        forward_x(xe)
    ring_step(1)
    forward_z(1)
    ring_step(2)
    forward_z(2)
    ring_step(3)
    ring_step(4)
    for yo, k, n in sibs:
        arrived(piece(yo, 1 - c, k), sib_s.at[n], sib_r.at[n])
    own.wait()

    acc[...] = jnp.zeros_like(acc)

    def multiply(i, carry):
        pe, xe = i // NX, i % NX
        s = slot(xe, pe)

        @pl.when(xe != 0)
        def _():
            arrived(zpart(s), wz_s.at[0], wz_r.at[s])

        @pl.when(pe != 0)
        def _():
            arrived(xpart(s), wx_s.at[0], wx_r.at[s])

        cols = pl.ds(pl.multiple_of(s * CHUNK, 128), CHUNK)
        acc[...] += jnp.dot(rall[:, cols], w[s], preferred_element_type=jnp.float32)
        return carry

    lax.fori_loop(0, SLOTS, multiply, 0)

    send(acc.at[pl.ds(ROWS, ROWS)], pin, p_s, p_r, mate)
    arrived(pin, p_s, p_r)
    projected = acc[0:ROWS] + pin[...]
    out[...] = projected.astype(out.dtype)

    def over_columns(v):
        return jnp.sum((v[:, :128] + v[:, 128:]).T, axis=0, keepdims=True)

    s0[...] = jnp.zeros_like(s0)
    s0[0:1] = over_columns(projected * projected)
    s0[1:2] = over_columns(projected * head[...].astype(jnp.float32))
    send(s0, s1, sc_s.at[0], sc_r.at[0], sibling)
    arrived(s1, sc_s.at[0], sc_r.at[0])
    ys[y] = s0[...] + s1[...]
    for e in range(1, NY):
        send(ys.at[y], ys.at[y], sc_s.at[e], sc_r.at[e], at_y(e))
    for e in range(1, NY):
        arrived(ys.at[(y - e + NY) % NY], sc_s.at[e], sc_r.at[e])
    z0[...] = jnp.sum(ys[...], axis=0)
    send(z0, z1, sc_s.at[NY], sc_r.at[NY], other)
    arrived(z1, sc_s.at[NY], sc_r.at[NY])
    total = z0[...] + z1[...]
    scores[...] = total[1:2] / jnp.sqrt(total[0:1] / D + 1e-06)

    for copy in sent:
        copy.wait_send()


def on_device(codes, offsets, responses, head):
    vmem = pl.BlockSpec(memory_space=pltpu.VMEM)
    dma = pltpu.SemaphoreType.DMA
    f32, bf16 = jnp.float32, jnp.bfloat16
    out, scores = pl.pallas_call(
        kernel,
        out_shape=(
            jax.ShapeDtypeStruct((ROWS, COLS), bf16),
            jax.ShapeDtypeStruct((1, ROWS), f32),
        ),
        in_specs=[vmem, vmem, pl.BlockSpec(memory_space=pl.ANY), vmem],
        out_specs=(vmem, vmem),
        scratch_shapes=[
            pltpu.VMEM((2 * ROWS, HALF), bf16),
            pltpu.VMEM((SLOTS, CHUNK, COLS), bf16),
            pltpu.VMEM((2 * ROWS, COLS), f32),
            pltpu.VMEM((ROWS, COLS), f32),
            pltpu.VMEM((8, ROWS), f32),
            pltpu.VMEM((8, ROWS), f32),
            pltpu.VMEM((NY, 8, ROWS), f32),
            pltpu.VMEM((8, ROWS), f32),
            pltpu.VMEM((8, ROWS), f32),
            dma,
            dma((2,)), dma((2,)),
            dma((16,)), dma((16,)),
            dma((16,)), dma((16,)),
            dma((12,)), dma((SLOTS,)),
            dma((12,)), dma((SLOTS,)),
            dma, dma,
            dma((NY + 1,)), dma((NY + 1,)),
        ],
        compiler_params=pltpu.CompilerParams(
            collective_id=0, has_side_effects=True, vmem_limit_bytes=60 * 2**20
        ),
        cost_estimate=pl.CostEstimate(flops=2 * ROWS * 2 * HALF * COLS, bytes_accessed=8 * 2**20, transcendentals=0),
        name="project_and_score",
    )(codes, offsets, responses, head.reshape(1, COLS))
    return out, scores.reshape(ROWS)


def solution(mesh):
    in_specs = (P("fsdp", "tp"), P("fsdp", "tp"), P("fsdp", None), P("tp"))
    out_specs = (P("fsdp", "tp"), P("fsdp"))
    return jax.shard_map(
        on_device, mesh=mesh, in_specs=in_specs, out_specs=out_specs, check_vma=False
    )
```

time: 320 us -> 96.4 us (0.30)
  the two profiles are of different devices: /device:TPU:1 before, /device:TPU:194 now
where the time goes in v1:
time: 96.4 us; the launch traced here: 96.2 us
  Pallas kernels  90.1 us (93%)
  local copies, waits for them, and re-layouts  5.37 us (6%)
    pallas_call x1, Pallas kernels, on_device(): pl.pallas_call(kernel, out_shape=(jax.ShapeDtypeStruct((ROWS, COLS), bf16...  90.1 us
    unnamed x3, local copies, waits for them, and re-layouts  4.15 us

profile of v1, /device:TPU:194, one launch (start us, length us, event | category | flops | bytes accessed | tf_op | source)
XLA Modules:
  0.0 96.2 jit_solution(16519530740851808816)
XLA Ops:
  0.6 1.2 %reshape.10.head = bf16[1,256]{1,0:T(2,128)(2,1)} reshape(bf16[256]{0:T(256)(128)(2,1)} %param.7) | data formatting | bytes 1024 | tf_op jit(solution)/shard_map/reshape | solution.py:269
  1.9 1.4 %copy.6.offsets = s32[5,2]{1,0:T(8,128)} copy(s32[5,2]{0,1:T(2,128)} %param.5) | data formatting | bytes 80 | tf_op args[1]
  3.2 90.1 %project_and_score.1 = (bf16[256,256]{1,0:T(8,128)(2,1)}, f32[1,256]{1,0:T(1,128)}) custom-call(bf16[640,256]{1,0:T(8,128)(2,1)} %codes.1, s32[5,2]{1,0:T(8,128)} %copy.6.offsets, bf16[256,15360]{1,0:T(8,128)(2,1)} %responses.1, bf16[1,256]{1,0:T(2,128)(2,1)} %reshape.10.head), custom_call_target="tpu_custom_call" | custom-call | flops 2013265920 | bytes 8388608 | tf_op jit(solution)/shard_map/project_and_score/pallas_call | solution.py:237
  93.4 1.6 %copy.9 = bf16[256,256]{1,0:T(8,128)(2,1)} copy(bf16[256,256]{1,0:T(8,128)(2,1)} %get-tuple-element.8) | data formatting | bytes 262144
  94.9 1.2 %copy.10 = f32[256]{0:T(256)} copy(f32[256]{0:T(256)} %bitcast.1) | data formatting | bytes 2048

commit v2 on v1

--- a/solution.py
+++ b/solution.py
@@ -14,7 +14,7 @@
 COLS = 256
 HALF = NX * NH * CHUNK
 SLOTS = NX * NH
-ZF = 512
+ZF = 464
 SUB = HALF // 2
 PIECE = ROWS // (2 * NY)
 
@@ -25,9 +25,9 @@
 
 def kernel(
     codes, offsets, responses, head, out, scores,
-    rall, w, acc, pin, s0, s1, ys, z0, z1,
+    rall, w, acc, pout, pin, kout, kin, s0, s1, ys,
     own_sem, inj_s, inj_r, ring_s, ring_r, sib_s, sib_r,
-    wz_s, wz_r, wx_s, wx_r, p_s, p_r, sc_s, sc_r,
+    wz_s, wz_r, wx_s, wx_r, p_s, p_r, k_s, k_r, sc_s, sc_r,
 ):
     f, t = lax.axis_index("fsdp"), lax.axis_index("tp")
     x, zl = f % NX, f // NX
@@ -45,18 +45,22 @@
     def at_y(e):
         return device(x, (y + e + NY) % NY, zl, zh, c)
 
-    z = zh * NZ + zl
-    near = jnp.where(zl < 2, z + 10, jnp.where(zl == 2, z + 1, jnp.where(zl == 3, z + 11, z + 2))) % (2 * NZ)
-    wants = device(x, y, near % NZ, near // NZ, c)
-    mate_zl = jnp.where(zl < 2, zl + 4, jnp.where(zl == 2, 3, jnp.where(zl == 3, 2, zl - 4)))
-    mate = device(x, y, mate_zl, zh, c)
-    other = device(x, y, zl, 1 - zh, c)
+    mate = device(x, y, NZ - 1 - zl, zh, c)
+    outer, middle = (zl == 0) | (zl == NZ - 1), (zl == NH - 1) | (zl == NH)
+    wants = [
+        device(x, y, NZ - 1 - zl, jnp.where(outer, 1 - zh, zh), c),
+        device(x, y, NZ - 1 - zl, jnp.where(middle, zh, 1 - zh), c),
+    ]
+    group = [(e, g) for g in range(2) for e in range(NY) if e or g]
+
+    def at_group(e, g):
+        return device(x, (y + e) % NY, zl, (zh + g) % 2, c)
 
     barrier = pltpu.get_barrier_semaphore()
-    partners = [sibling, wants, mate, other]
+    partners = [sibling, mate, *wants]
     partners += [at_x(e) for e in range(1, NX)]
     partners += [at_z(e) for e in range(1, NH)]
-    partners += [at_y(e) for e in range(1, NY)]
+    partners += [at_group(e, g) for e, g in group]
     for partner in partners:
         pl.semaphore_signal(barrier, inc=1, device_id=partner, device_id_type=MESH)
 
@@ -75,7 +79,7 @@
         for j in range(COLS // BLK):
             block = codes[i * BLK : (i + 1) * BLK, j * BLK : (j + 1) * BLK].astype(jnp.float32)
             amax = jnp.max(jnp.max(jnp.abs(block), axis=0, keepdims=True), axis=1, keepdims=True)
-            scale = jnp.exp2(offsets[i : i + 1, j : j + 1].astype(jnp.float32)) / (amax + 1e-06)
+            scale = jnp.exp2(offsets[j : j + 1, i : i + 1].astype(jnp.float32)) / (amax + 1e-06)
             w[mine, i * BLK : (i + 1) * BLK, j * BLK : (j + 1) * BLK] = (block * scale).astype(jnp.bfloat16)
 
     pl.semaphore_wait(barrier, len(partners))
@@ -120,15 +124,16 @@
         col = pl.multiple_of((1 - h) * HALF + k * SUB, 128)
         send(
             responses.at[pl.ds(row, PIECE), pl.ds(col, SUB)],
-            piece(y, c, k), inj_s.at[k], inj_r.at[k], wants,
+            piece(y, c, k), inj_s.at[k], inj_r.at[k], wants[k],
         )
-    for e in range(1, NX):
+    first = jnp.where(p == NH - 1, 2, 1)
+    for e in (1, 3, 2):
         send_w("wx", mine, at_x(e))
-    for e in range(1, NH):
+    for e in (first, NH - first):
         send_w("wz", mine, at_z(e))
-    for e in range(1, NX):
+    for e in (1, 3, 2):
         send_w("wz", mine, at_x(e))
-    for e in range(1, NH):
+    for e in (first, NH - first):
         send_w("wx", mine, at_z(e))
 
     def ring(dir_, k, d):
@@ -148,36 +153,41 @@
 
     sibs = []
 
-    def ring_step(d):
-        for k in range(2):
-            for dir_ in (1, -1):
-                if d <= (4 if (dir_ == 1) == (k == 0) else 3):
-                    ring(dir_, k, d)
+    def ring_step(d, k):
+        for dir_ in (1, -1):
+            if d <= (4 if (dir_ == 1) == (k == 0) else 3):
+                ring(dir_, k, d)
 
     def forward_x(xe):
         s = slot(xe, 0)
         arrived(xpart(s), wx_s.at[0], wx_r.at[s])
-        for e in range(1, NH):
+        for e in (first, NH - first):
             send_w("wx", s, at_z(e))
 
     def forward_z(pe):
         s = slot(0, pe)
         arrived(zpart(s), wz_s.at[0], wz_r.at[s])
-        for e in range(1, NX):
+        for e in (1, 3, 2):
             send_w("wz", s, at_x(e))
 
-    for k in range(2):
+    def ring_start(k):
         arrived(piece(y, c, k), inj_s.at[k], inj_r.at[k])
         ring(1, k, 0)
         ring(-1, k, 0)
+
+    ring_start(0)
     for xe in (1, 3, 2):
         forward_x(xe)
-    ring_step(1)
-    forward_z(1)
-    ring_step(2)
-    forward_z(2)
-    ring_step(3)
-    ring_step(4)
+    ring_start(1)
+    ring_step(1, 0)
+    forward_z(first)
+    ring_step(1, 1)
+    ring_step(2, 0)
+    forward_z(NH - first)
+    ring_step(2, 1)
+    for d in (3, 4):
+        for k in range(2):
+            ring_step(d, k)
     for yo, k, n in sibs:
         arrived(piece(yo, 1 - c, k), sib_s.at[n], sib_r.at[n])
     own.wait()
@@ -185,7 +195,8 @@
     acc[...] = jnp.zeros_like(acc)
 
     def multiply(i, carry):
-        pe, xe = i // NX, i % NX
+        step, xe = i // NX, i % NX
+        pe = step * first % NH
         s = slot(xe, pe)
 
         @pl.when(xe != 0)
@@ -202,32 +213,41 @@
 
     lax.fori_loop(0, SLOTS, multiply, 0)
 
-    send(acc.at[pl.ds(ROWS, ROWS)], pin, p_s, p_r, mate)
+    part = acc[ROWS:]
+    amax = jnp.max(jnp.max(jnp.abs(part), axis=0, keepdims=True), axis=1, keepdims=True)
+    unit = jnp.maximum(amax, 1e-30) / 32760.0
+    pout[...] = jnp.floor(part * (1.0 / unit) + 0.5).astype(jnp.int32).astype(jnp.int16)
+    kout[...] = jnp.broadcast_to(unit, kout.shape)
+    send(pout, pin, p_s, p_r, mate)
+    send(kout, kin, k_s, k_r, mate)
     arrived(pin, p_s, p_r)
-    projected = acc[0:ROWS] + pin[...]
+    arrived(kin, k_s, k_r)
+    projected = acc[:ROWS] + pin[...].astype(jnp.int32).astype(jnp.float32) * kin[0:1, 0:1]
     out[...] = projected.astype(out.dtype)
 
     def over_columns(v):
         return jnp.sum((v[:, :128] + v[:, 128:]).T, axis=0, keepdims=True)
 
-    s0[...] = jnp.zeros_like(s0)
     s0[0:1] = over_columns(projected * projected)
-    s0[1:2] = over_columns(projected * head[...].astype(jnp.float32))
+    s0[1:2] = over_columns(projected * head[...].astype(jnp.float32).reshape(1, COLS))
     send(s0, s1, sc_s.at[0], sc_r.at[0], sibling)
     arrived(s1, sc_s.at[0], sc_r.at[0])
-    ys[y] = s0[...] + s1[...]
-    for e in range(1, NY):
-        send(ys.at[y], ys.at[y], sc_s.at[e], sc_r.at[e], at_y(e))
-    for e in range(1, NY):
-        arrived(ys.at[(y - e + NY) % NY], sc_s.at[e], sc_r.at[e])
-    z0[...] = jnp.sum(ys[...], axis=0)
-    send(z0, z1, sc_s.at[NY], sc_r.at[NY], other)
-    arrived(z1, sc_s.at[NY], sc_r.at[NY])
-    total = z0[...] + z1[...]
+    here = zh * NY + y
+    ys[here] = s0[...] + s1[...]
+    for n, (e, g) in enumerate(group, 1):
+        send(ys.at[here], ys.at[here], sc_s.at[n], sc_r.at[n], at_group(e, g))
+    for n, (e, g) in enumerate(group, 1):
+        arrived(ys.at[(zh + g) % 2 * NY + (y - e + NY) % NY], sc_s.at[n], sc_r.at[n])
+    total = jnp.sum(ys[...], axis=0)
     scores[...] = total[1:2] / jnp.sqrt(total[0:1] / D + 1e-06)
 
     for copy in sent:
         copy.wait_send()
+
+
+def results(out_in, scores_in, out, scores):
+    out[...] = out_in[...]
+    scores[...] = scores_in[...]
 
 
 def on_device(codes, offsets, responses, head):
@@ -246,12 +266,13 @@
             pltpu.VMEM((2 * ROWS, HALF), bf16),
             pltpu.VMEM((SLOTS, CHUNK, COLS), bf16),
             pltpu.VMEM((2 * ROWS, COLS), f32),
-            pltpu.VMEM((ROWS, COLS), f32),
-            pltpu.VMEM((8, ROWS), f32),
-            pltpu.VMEM((8, ROWS), f32),
-            pltpu.VMEM((NY, 8, ROWS), f32),
-            pltpu.VMEM((8, ROWS), f32),
-            pltpu.VMEM((8, ROWS), f32),
+            pltpu.VMEM((ROWS, COLS), jnp.int16),
+            pltpu.VMEM((ROWS, COLS), jnp.int16),
+            pltpu.VMEM((8, 128), f32),
+            pltpu.VMEM((8, 128), f32),
+            pltpu.VMEM((2, ROWS), f32),
+            pltpu.VMEM((2, ROWS), f32),
+            pltpu.VMEM((2 * NY, 2, ROWS), f32),
             dma,
             dma((2,)), dma((2,)),
             dma((16,)), dma((16,)),
@@ -259,14 +280,23 @@
             dma((12,)), dma((SLOTS,)),
             dma((12,)), dma((SLOTS,)),
             dma, dma,
-            dma((NY + 1,)), dma((NY + 1,)),
+            dma, dma,
+            dma((2 * NY,)), dma((2 * NY,)),
         ],
         compiler_params=pltpu.CompilerParams(
             collective_id=0, has_side_effects=True, vmem_limit_bytes=60 * 2**20
         ),
         cost_estimate=pl.CostEstimate(flops=2 * ROWS * 2 * HALF * COLS, bytes_accessed=8 * 2**20, transcendentals=0),
         name="project_and_score",
-    )(codes, offsets, responses, head.reshape(1, COLS))
+    )(codes, offsets.T, responses, head)
+    out, scores = pl.pallas_call(
+        results,
+        out_shape=(
+            jax.ShapeDtypeStruct((ROWS, COLS), bf16),
+            jax.ShapeDtypeStruct((1, ROWS), f32),
+        ),
+        name="results",
+    )(out, scores)
     return out, scores.reshape(ROWS)
 
 

time: 96.4 us -> 78.3 us (0.81)
  the two profiles are of different devices: /device:TPU:194 before, /device:TPU:1 now
where the time goes in v2:
time: 78.3 us; the launch traced here: 78.1 us
  Pallas kernels  77.5 us (99%)
    pallas_call x1, Pallas kernels, on_device(): pl.pallas_call(kernel, out_shape=(jax.ShapeDtypeStruct((ROWS, COLS), bf16...  75.9 us
    pallas_call x1, Pallas kernels, on_device(): pl.pallas_call(results, out_shape=(jax.ShapeDtypeStruct((ROWS, COLS), bf1...  1.57 us

profile of v2, /device:TPU:1, one launch (start us, length us, event | category | flops | bytes accessed | tf_op | source)
XLA Modules:
  0.0 78.1 jit_solution(7694772653904199297)
XLA Ops:
  0.6 75.9 %project_and_score.1 = (bf16[256,256]{1,0:T(8,128)(2,1)}, f32[1,256]{1,0:T(1,128)}) custom-call(bf16[640,256]{1,0:T(8,128)(2,1)} %codes.1, s32[2,5]{1,0:T(2,128)} %bitcast.2, bf16[256,15360]{1,0:T(8,128)(2,1)} %responses.1, bf16[256]{0:T(256)(128)(2,1)} %head.1), custom_call_target="tpu_custom_call" | custom-call | flops 2013265920 | bytes 8388608 | tf_op jit(solution)/shard_map/project_and_score/pallas_call | solution.py:257
  76.5 1.6 %results.1 = (bf16[256,256]{1,0:T(8,128)(2,1)}, f32[1,256]{1,0:T(1,128)}) custom-call(bf16[256,256]{1,0:T(8,128)(2,1)} %get-tuple-element.6.out_in, f32[1,256]{1,0:T(1,128)} %get-tuple-element.7.scores_in), custom_call_target="tpu_custom_call" | custom-call | tf_op jit(solution)/shard_map/results/pallas_call | solution.py:292

commit v3 on v2

v3 whole, which is shorter than its diff:
```python
import jax
import jax.numpy as jnp
from jax import lax
from jax.experimental import pallas as pl
from jax.experimental.pallas import tpu as pltpu
from jax.sharding import PartitionSpec as P

MESH = pl.DeviceIdType.MESH
BLK = 128
D = 8192
NX, NY, NZ, NH = 4, 8, 6, 3
ROWS = 256
CHUNK = 640
COLS = 256
HALF = NX * NH * CHUNK
SLOTS = NX * NH
ZF = 464
PARTS = ((0, ZF), (0, 240), (240, ZF - 240), (ZF, CHUNK - ZF), (ZF, 96), (ZF + 96, CHUNK - ZF - 96))
ZALL, ZTOP, ZLOW, XALL, XTOP, XLOW = range(len(PARTS))
SUBS = 4
SUB = HALF // SUBS
PIECE = ROWS // (2 * NY)


def device(x, y, zl, zh, c):
    return (zl * NX + x, (zh * NY + y) * 2 + c)


def kernel(
    codes, offsets, responses, head, out, scores,
    rall, w, acc, pout, pin, kout, kin, ys, zs,
    own_sem, inj_s, inj_r, ring_s, ring_r, sib_s, sib_r,
    w_s, w_r, p_s, p_r, k_s, k_r, sc_s, sc_r,
):
    f, t = lax.axis_index("fsdp"), lax.axis_index("tp")
    x, zl = f % NX, f // NX
    c, y, zh = t % 2, (t // 2) % NY, t // (2 * NY)
    h, p = zl // NH, zl % NH

    sibling = device(x, y, zl, zh, 1 - c)

    def at_x(e):
        return device((x + e) % NX, y, zl, zh, c)

    def at_z(e):
        return device(x, y, h * NH + (p + e) % NH, zh, c)

    def at_y(e):
        return device(x, (y + e + NY) % NY, zl, zh, c)

    mate = device(x, y, NZ - 1 - zl, zh, c)
    outer, middle = (zl == 0) | (zl == NZ - 1), (zl == NH - 1) | (zl == NH)
    wants = [
        device(x, y, NZ - 1 - zl, jnp.where(outer, 1 - zh, zh), c),
        device(x, y, NZ - 1 - zl, jnp.where(middle, zh, 1 - zh), c),
    ]
    rest = [device(x, y, zl, (zh + g) % 2, (c + k) % 2) for g, k in ((0, 1), (1, 0), (1, 1))]

    barrier = pltpu.get_barrier_semaphore()
    partners = [mate, *wants, *rest, at_x(1), at_x(3)]
    partners += [at_z(e) for e in range(1, NH)]
    partners += [at_y(e) for e in range(1, NY)]
    for partner in partners:
        pl.semaphore_signal(barrier, inc=1, device_id=partner, device_id_type=MESH)

    own = pltpu.make_async_copy(
        responses.at[:, pl.ds(pl.multiple_of(h * HALF, 128), HALF)],
        rall.at[pl.ds(0, ROWS)],
        own_sem,
    )
    own.start()

    def slot(xe, pe):
        return ((p + pe) % NH) * NX + (x + xe) % NX

    mine = slot(0, 0)
    for i in range(CHUNK // BLK):
        for j in range(COLS // BLK):
            block = codes[i * BLK : (i + 1) * BLK, j * BLK : (j + 1) * BLK].astype(jnp.float32)
            amax = jnp.max(jnp.max(jnp.abs(block), axis=0, keepdims=True), axis=1, keepdims=True)
            scale = jnp.exp2(offsets[j : j + 1, i : i + 1].astype(jnp.float32)) / (amax + 1e-06)
            w[mine, i * BLK : (i + 1) * BLK, j * BLK : (j + 1) * BLK] = (block * scale).astype(jnp.bfloat16)

    pl.semaphore_wait(barrier, len(partners))

    sent = []

    def send(src, dst, send_sem, recv_sem, to):
        copy = pltpu.make_async_remote_copy(
            src_ref=src, dst_ref=dst, send_sem=send_sem, recv_sem=recv_sem,
            device_id=to, device_id_type=MESH,
        )
        copy.start()
        sent.append(copy)

    def arrived(dst, send_sem, recv_sem):
        pltpu.make_async_remote_copy(
            src_ref=dst, dst_ref=dst, send_sem=send_sem, recv_sem=recv_sem,
            device_id=sibling, device_id_type=MESH,
        ).wait_recv()

    def piece(yo, core, k):
        row = pl.multiple_of(ROWS + 2 * PIECE * yo + PIECE * core, PIECE)
        return rall.at[pl.ds(row, PIECE), pl.ds(k * SUB, SUB)]

    def part(kind, s):
        row, rows = PARTS[kind]
        return w.at[s, pl.ds(row, rows)]

    count = {"w": 0, "ring": 0}

    def send_w(kind, s, to):
        n = count["w"]
        count["w"] += 1
        send(part(kind, s), part(kind, s), w_s.at[n], w_r.at[kind, s], to)

    def arrived_w(kind, s):
        arrived(part(kind, s), w_s.at[0], w_r.at[kind, s])

    def send_rows(k):
        row = pl.multiple_of(2 * PIECE * y + PIECE * c, PIECE)
        col = pl.multiple_of((1 - h) * HALF + k * SUB, 128)
        send(
            responses.at[pl.ds(row, PIECE), pl.ds(col, SUB)],
            piece(y, c, k), inj_s.at[k], inj_r.at[k], wants[k % 2],
        )

    near = jnp.where(p == NH - 1, 2, 1)
    far = NH - near

    send_rows(0)
    send_rows(1)
    for e in (1, 3):
        send_w(XALL, mine, at_x(e))
    for e in (near, far):
        send_w(ZALL, mine, at_z(e))
    for e in (1, 3):
        send_w(ZALL, mine, at_x(e))
    send_rows(2)
    send_rows(3)
    for e in (near, far):
        send_w(XALL, mine, at_z(e))

    sibs = []

    def steps(dir_, k):
        return 4 if (dir_ == 1) == (k % 2 == 0) else 3

    def ring(dir_, k, d):
        yo = (y - dir_ * d + NY) % NY
        ref = piece(yo, c, k)
        i = ((0 if dir_ == 1 else 1) * SUBS + k) * 4
        if d > 0:
            arrived(ref, ring_s.at[i + d - 1], ring_r.at[i + d - 1])
        if d < steps(dir_, k):
            send(ref, ref, ring_s.at[i + d], ring_r.at[i + d], at_y(dir_))
        if d > 0 or dir_ == 1:
            n = count["ring"]
            count["ring"] += 1
            send(ref, ref, sib_s.at[n], sib_r.at[n], sibling)
            sibs.append((yo, k, n))

    def ring_start(*ks):
        for k in ks:
            arrived(piece(y, c, k), inj_s.at[k], inj_r.at[k])
            ring(1, k, 0)
            ring(-1, k, 0)

    def ring_step(d, *ks):
        for k in ks:
            for dir_ in (1, -1):
                if d <= steps(dir_, k):
                    ring(dir_, k, d)

    def pass_x(whole, top, low, pe):
        for xe, half, to in ((1, low, 3), (3, top, 1)):
            arrived_w(whole, slot(xe, pe))
            send_w(half, slot(xe, pe), at_x(to))

    def turn_z(xe):
        for e in (near, far):
            send_w(XALL, slot(xe, 0), at_z(e))

    def turn_x(pe):
        arrived_w(ZALL, slot(0, pe))
        for e in (1, 3):
            send_w(ZALL, slot(0, pe), at_x(e))

    pass_x(XALL, XTOP, XLOW, 0)
    turn_z(1)
    turn_z(3)
    ring_start(0, 1)
    ring_step(1, 0, 1)
    turn_x(near)
    ring_start(2, 3)
    ring_step(2, 0, 1)
    pass_x(ZALL, ZTOP, ZLOW, 0)
    ring_step(1, 2, 3)
    arrived_w(XTOP, slot(2, 0))
    arrived_w(XLOW, slot(2, 0))
    turn_z(2)
    ring_step(3, 0, 1)
    turn_x(far)
    ring_step(2, 2, 3)
    pass_x(ZALL, ZTOP, ZLOW, near)
    ring_step(4, 0, 1)
    ring_step(3, 2, 3)
    pass_x(ZALL, ZTOP, ZLOW, far)
    ring_step(4, 2, 3)
    for yo, k, n in sibs:
        arrived(piece(yo, 1 - c, k), sib_s.at[n], sib_r.at[n])
    own.wait()

    acc[...] = jnp.zeros_like(acc)

    def multiply(i, carry):
        step, xe = i // NX, i % NX
        xe = jnp.where(xe < 2, xe, 5 - xe)
        s = slot(xe, step * near % NH)

        @pl.when(xe == 2)
        def _():
            arrived_w(ZTOP, s)
            arrived_w(ZLOW, s)

        @pl.when(step != 0)
        def _():
            arrived_w(XALL, s)

        cols = pl.ds(pl.multiple_of(s * CHUNK, 128), CHUNK)
        acc[...] += jnp.dot(rall[:, cols], w[s], preferred_element_type=jnp.float32)
        return carry

    lax.fori_loop(0, SLOTS, multiply, 0)

    sums = acc[ROWS:]
    amax = jnp.max(jnp.max(jnp.abs(sums), axis=0, keepdims=True), axis=1, keepdims=True)
    unit = jnp.maximum(amax, 1e-30) / 32760.0
    pout[...] = jnp.floor(sums * (1.0 / unit) + 0.5).astype(jnp.int32).astype(jnp.int16)
    kout[...] = jnp.broadcast_to(unit, kout.shape)
    send(pout, pin, p_s, p_r, mate)
    send(kout, kin, k_s, k_r, mate)
    arrived(pin, p_s, p_r)
    arrived(kin, k_s, k_r)
    projected = acc[:ROWS] + pin[...].astype(jnp.int32).astype(jnp.float32) * kin[0:1, 0:1]
    out[...] = projected.astype(out.dtype)

    def over_columns(v):
        return jnp.sum((v[:, :128] + v[:, 128:]).T, axis=0, keepdims=True)

    ys[y, 0:1] = over_columns(projected * projected)
    ys[y, 1:2] = over_columns(projected * head[...].astype(jnp.float32).reshape(1, COLS))
    for e in range(1, NY):
        send(ys.at[y], ys.at[y], sc_s.at[e], sc_r.at[e], at_y(e))
    for e in range(1, NY):
        arrived(ys.at[(y - e + NY) % NY], sc_s.at[e], sc_r.at[e])
    here = zh * 2 + c
    zs[here] = jnp.sum(ys[...], axis=0)
    for n, to in enumerate(rest):
        send(zs.at[here], zs.at[here], sc_s.at[NY + n], sc_r.at[NY + n], to)
    for n, (g, k) in enumerate(((0, 1), (1, 0), (1, 1))):
        arrived(zs.at[(zh + g) % 2 * 2 + (c + k) % 2], sc_s.at[NY + n], sc_r.at[NY + n])
    total = jnp.sum(zs[...], axis=0)
    scores[...] = total[1:2] / jnp.sqrt(total[0:1] / D + 1e-06)

    for copy in sent:
        copy.wait_send()


def results(out_in, scores_in, out, scores):
    out[...] = out_in[...]
    scores[...] = scores_in[...]


def on_device(codes, offsets, responses, head):
    vmem = pl.BlockSpec(memory_space=pltpu.VMEM)
    dma = pltpu.SemaphoreType.DMA
    f32, bf16 = jnp.float32, jnp.bfloat16
    out, scores = pl.pallas_call(
        kernel,
        out_shape=(
            jax.ShapeDtypeStruct((ROWS, COLS), bf16),
            jax.ShapeDtypeStruct((1, ROWS), f32),
        ),
        in_specs=[vmem, vmem, pl.BlockSpec(memory_space=pl.ANY), vmem],
        out_specs=(vmem, vmem),
        scratch_shapes=[
            pltpu.VMEM((2 * ROWS, HALF), bf16),
            pltpu.VMEM((SLOTS, CHUNK, COLS), bf16),
            pltpu.VMEM((2 * ROWS, COLS), f32),
            pltpu.VMEM((ROWS, COLS), jnp.int16),
            pltpu.VMEM((ROWS, COLS), jnp.int16),
            pltpu.VMEM((8, 128), f32),
            pltpu.VMEM((8, 128), f32),
            pltpu.VMEM((NY, 2, ROWS), f32),
            pltpu.VMEM((4, 2, ROWS), f32),
            dma,
            dma((SUBS,)), dma((SUBS,)),
            dma((8 * SUBS,)), dma((8 * SUBS,)),
            dma((8 * SUBS,)), dma((8 * SUBS,)),
            dma((2 * SLOTS + 4,)), dma((len(PARTS), SLOTS)),
            dma, dma,
            dma, dma,
            dma((NY + 3,)), dma((NY + 3,)),
        ],
        compiler_params=pltpu.CompilerParams(
            collective_id=0, has_side_effects=True, vmem_limit_bytes=60 * 2**20
        ),
        cost_estimate=pl.CostEstimate(flops=2 * ROWS * 2 * HALF * COLS, bytes_accessed=8 * 2**20, transcendentals=0),
        name="project_and_score",
    )(codes, offsets.T, responses, head)
    out, scores = pl.pallas_call(
        results,
        out_shape=(
            jax.ShapeDtypeStruct((ROWS, COLS), bf16),
            jax.ShapeDtypeStruct((1, ROWS), f32),
        ),
        name="results",
    )(out, scores)
    return out, scores.reshape(ROWS)


def solution(mesh):
    in_specs = (P("fsdp", "tp"), P("fsdp", "tp"), P("fsdp", None), P("tp"))
    out_specs = (P("fsdp", "tp"), P("fsdp"))
    return jax.shard_map(
        on_device, mesh=mesh, in_specs=in_specs, out_specs=out_specs, check_vma=False
    )
```

time: 78.3 us -> 78.2 us (level)
  no operation moved by 1% of the time
where the time goes in v3:
time: 78.2 us; the launch traced here: 78 us
  Pallas kernels  77.4 us (99%)
    pallas_call x1, Pallas kernels, on_device(): pl.pallas_call(kernel, out_shape=(jax.ShapeDtypeStruct((ROWS, COLS), bf16...  75.8 us
    pallas_call x1, Pallas kernels, on_device(): pl.pallas_call(results, out_shape=(jax.ShapeDtypeStruct((ROWS, COLS), bf1...  1.57 us

profile of v3, /device:TPU:1, one launch (start us, length us, event | category | flops | bytes accessed | tf_op | source)
XLA Modules:
  0.0 78.0 jit_solution(10675840029013079912)
XLA Ops:
  0.6 75.8 %project_and_score.1 = (bf16[256,256]{1,0:T(8,128)(2,1)}, f32[1,256]{1,0:T(1,128)}) custom-call(bf16[640,256]{1,0:T(8,128)(2,1)} %codes.1, s32[2,5]{1,0:T(2,128)} %bitcast.2, bf16[256,15360]{1,0:T(8,128)(2,1)} %responses.1, bf16[256]{0:T(256)(128)(2,1)} %head.1), custom_call_target="tpu_custom_call" | custom-call | flops 2013265920 | bytes 8388608 | tf_op jit(solution)/shard_map/project_and_score/pallas_call | solution.py:279
  76.4 1.6 %results.1 = (bf16[256,256]{1,0:T(8,128)(2,1)}, f32[1,256]{1,0:T(1,128)}) custom-call(bf16[256,256]{1,0:T(8,128)(2,1)} %get-tuple-element.6.out_in, f32[1,256]{1,0:T(1,128)} %get-tuple-element.7.scores_in), custom_call_target="tpu_custom_call" | custom-call | tf_op jit(solution)/shard_map/results/pallas_call | solution.py:312

commit v4 on v3

--- a/solution.py
+++ b/solution.py
@@ -14,12 +14,31 @@
 COLS = 256
 HALF = NX * NH * CHUNK
 SLOTS = NX * NH
-ZF = 464
-PARTS = ((0, ZF), (0, 240), (240, ZF - 240), (ZF, CHUNK - ZF), (ZF, 96), (ZF + 96, CHUNK - ZF - 96))
+ZF = 496
+ZT, XT = (ZF // 2 + 15) // 16 * 16, ((CHUNK - ZF) // 2 + 15) // 16 * 16
+PARTS = ((0, ZF), (0, ZT), (ZT, ZF - ZT), (ZF, CHUNK - ZF), (ZF, XT), (ZF + XT, CHUNK - ZF - XT))
 ZALL, ZTOP, ZLOW, XALL, XTOP, XLOW = range(len(PARTS))
 SUBS = 4
 SUB = HALF // SUBS
 PIECE = ROWS // (2 * NY)
+PLANE = NX * CHUNK
+ORDER = (
+    ("rows", 0), ("x", XALL, 1), ("x", ZALL, 1), ("rows", 1),
+    ("z", ZALL, "near"), ("x", ZALL, 3), ("rows", 2), ("rows", 3),
+    ("z", ZALL, "far"), ("start", 0), ("x", XALL, 3), ("start", 1),
+    ("pass", ZALL, "own", 3), ("pass", ZALL, "own", 1), ("ring", -1, 1, 1), ("ring", 1, 0, 1),
+    ("ring", 1, 1, 1), ("ring", -1, 0, 1), ("pass", XALL, "own", 3), ("start", 2),
+    ("turn_x", "near"), ("ring", -1, 0, 2), ("ring", 1, 0, 2), ("turn_z", 3),
+    ("turn_z", 0), ("turn_z", 1), ("ring", 1, 2, 1), ("start", 3),
+    ("ring", -1, 1, 2), ("ring", 1, 2, 2), ("pass", XALL, "own", 1), ("ring", -1, 3, 1),
+    ("ring", 1, 0, 3), ("ring", -1, 2, 1), ("ring", 1, 1, 2), ("turn_x", "far"),
+    ("ring", 1, 3, 1), ("pass", ZALL, "near", 3), ("ring", 1, 2, 3), ("ring", -1, 3, 2),
+    ("ring", -1, 1, 3), ("ring", 1, 0, 4), ("ring", -1, 3, 3), ("ring", -1, 2, 2),
+    ("ring", 1, 3, 2), ("ring", -1, 1, 4), ("pass", ZALL, "near", 1), ("turn_z", 2),
+    ("product",), ("ring", 1, 2, 4), ("ring", -1, 0, 3), ("pass", ZALL, "far", 3),
+    ("pass", ZALL, "far", 1), ("ring", 1, 3, 3), ("ring", -1, 3, 4), ("ring", -1, 2, 3),
+    ("ring", 1, 1, 3),
+)
 
 
 def device(x, y, zl, zh, c):
@@ -27,7 +46,8 @@
 
 
 def kernel(
-    codes, offsets, responses, head, out, scores,
+    codes_in, offsets_in, responses, head_in, out, scores,
+    codes, offsets, head, projected_out, in_sem, out_sem,
     rall, w, acc, pout, pin, kout, kin, ys, zs,
     own_sem, inj_s, inj_r, ring_s, ring_r, sib_s, sib_r,
     w_s, w_r, p_s, p_r, k_s, k_r, sc_s, sc_r,
@@ -63,6 +83,12 @@
     for partner in partners:
         pl.semaphore_signal(barrier, inc=1, device_id=partner, device_id_type=MESH)
 
+    inputs = [
+        pltpu.make_async_copy(src, dst, in_sem.at[n])
+        for n, (src, dst) in enumerate(((codes_in, codes), (offsets_in, offsets), (head_in, head)))
+    ]
+    for copy in inputs:
+        copy.start()
     own = pltpu.make_async_copy(
         responses.at[:, pl.ds(pl.multiple_of(h * HALF, 128), HALF)],
         rall.at[pl.ds(0, ROWS)],
@@ -74,6 +100,8 @@
         return ((p + pe) % NH) * NX + (x + xe) % NX
 
     mine = slot(0, 0)
+    for copy in inputs:
+        copy.wait()
     for i in range(CHUNK // BLK):
         for j in range(COLS // BLK):
             block = codes[i * BLK : (i + 1) * BLK, j * BLK : (j + 1) * BLK].astype(jnp.float32)
@@ -114,8 +142,13 @@
         count["w"] += 1
         send(part(kind, s), part(kind, s), w_s.at[n], w_r.at[kind, s], to)
 
-    def arrived_w(kind, s):
-        arrived(part(kind, s), w_s.at[0], w_r.at[kind, s])
+    met = set()
+
+    def arrived_w(kind, xe, plane):
+        if (kind, xe, plane) not in met:
+            met.add((kind, xe, plane))
+            s = slot(xe, planes[plane])
+            arrived(part(kind, s), w_s.at[0], w_r.at[kind, s])
 
     def send_rows(k):
         row = pl.multiple_of(2 * PIECE * y + PIECE * c, PIECE)
@@ -128,19 +161,7 @@
     near = jnp.where(p == NH - 1, 2, 1)
     far = NH - near
 
-    send_rows(0)
-    send_rows(1)
-    for e in (1, 3):
-        send_w(XALL, mine, at_x(e))
-    for e in (near, far):
-        send_w(ZALL, mine, at_z(e))
-    for e in (1, 3):
-        send_w(ZALL, mine, at_x(e))
-    send_rows(2)
-    send_rows(3)
-    for e in (near, far):
-        send_w(XALL, mine, at_z(e))
-
+    planes = {"own": 0, "near": near, "far": far}
     sibs = []
 
     def steps(dir_, k):
@@ -160,78 +181,64 @@
             send(ref, ref, sib_s.at[n], sib_r.at[n], sibling)
             sibs.append((yo, k, n))
 
-    def ring_start(*ks):
-        for k in ks:
-            arrived(piece(y, c, k), inj_s.at[k], inj_r.at[k])
-            ring(1, k, 0)
-            ring(-1, k, 0)
-
-    def ring_step(d, *ks):
-        for k in ks:
-            for dir_ in (1, -1):
-                if d <= steps(dir_, k):
-                    ring(dir_, k, d)
-
-    def pass_x(whole, top, low, pe):
-        for xe, half, to in ((1, low, 3), (3, top, 1)):
-            arrived_w(whole, slot(xe, pe))
-            send_w(half, slot(xe, pe), at_x(to))
+    def ring_start(k):
+        arrived(piece(y, c, k), inj_s.at[k], inj_r.at[k])
+        ring(1, k, 0)
+        ring(-1, k, 0)
+
+    def start_x(kind, to):
+        send_w(kind, mine, at_x(to))
+
+    def start_z(kind, plane):
+        send_w(kind, mine, at_z(planes[plane]))
+
+    def pass_x(kind, plane, xe):
+        arrived_w(kind, xe, plane)
+        half = {(XALL, 1): XLOW, (XALL, 3): XTOP, (ZALL, 1): ZLOW, (ZALL, 3): ZTOP}[kind, xe]
+        send_w(half, slot(xe, planes[plane]), at_x(NX - xe))
 
     def turn_z(xe):
-        for e in (near, far):
-            send_w(XALL, slot(xe, 0), at_z(e))
-
-    def turn_x(pe):
-        arrived_w(ZALL, slot(0, pe))
-        for e in (1, 3):
-            send_w(ZALL, slot(0, pe), at_x(e))
-
-    pass_x(XALL, XTOP, XLOW, 0)
-    turn_z(1)
-    turn_z(3)
-    ring_start(0, 1)
-    ring_step(1, 0, 1)
-    turn_x(near)
-    ring_start(2, 3)
-    ring_step(2, 0, 1)
-    pass_x(ZALL, ZTOP, ZLOW, 0)
-    ring_step(1, 2, 3)
-    arrived_w(XTOP, slot(2, 0))
-    arrived_w(XLOW, slot(2, 0))
-    turn_z(2)
-    ring_step(3, 0, 1)
-    turn_x(far)
-    ring_step(2, 2, 3)
-    pass_x(ZALL, ZTOP, ZLOW, near)
-    ring_step(4, 0, 1)
-    ring_step(3, 2, 3)
-    pass_x(ZALL, ZTOP, ZLOW, far)
-    ring_step(4, 2, 3)
+        if xe:
+            for kind in (XTOP, XLOW) if xe == 2 else (XALL,):
+                arrived_w(kind, xe, "own")
+        for plane in ("near", "far"):
+            send_w(XALL, slot(xe, 0), at_z(planes[plane]))
+
+    def turn_x(plane):
+        arrived_w(ZALL, 0, plane)
+        for to in (1, 3):
+            send_w(ZALL, slot(0, planes[plane]), at_x(to))
+
+    def whole_plane(plane):
+        for xe in range(NX):
+            if xe or plane != "own":
+                for kind in (ZTOP, ZLOW) if xe == 2 else (ZALL,):
+                    arrived_w(kind, xe, plane)
+                for kind in (XTOP, XLOW) if xe == 2 and plane == "own" else (XALL,):
+                    arrived_w(kind, xe, plane)
+        return (p + planes[plane]) % NH
+
+    def product(first, rows, q):
+        cols = pl.ds(pl.multiple_of(q * PLANE, 128), PLANE)
+        weights = w[pl.ds(q * NX, NX)].reshape(PLANE, COLS)
+        return jnp.dot(rall[pl.ds(first, rows), cols], weights, preferred_element_type=jnp.float32)
+
+    def own_rows():
+        own.wait()
+        acc[:ROWS] = product(0, ROWS, whole_plane("own"))
+
+    steps_of = {
+        "rows": send_rows, "start": ring_start, "ring": ring, "x": start_x, "z": start_z,
+        "pass": pass_x, "turn_z": turn_z, "turn_x": turn_x, "product": own_rows,
+    }
+    for name, *what in ORDER:
+        steps_of[name](*what)
+
     for yo, k, n in sibs:
         arrived(piece(yo, 1 - c, k), sib_s.at[n], sib_r.at[n])
-    own.wait()
-
-    acc[...] = jnp.zeros_like(acc)
-
-    def multiply(i, carry):
-        step, xe = i // NX, i % NX
-        xe = jnp.where(xe < 2, xe, 5 - xe)
-        s = slot(xe, step * near % NH)
-
-        @pl.when(xe == 2)
-        def _():
-            arrived_w(ZTOP, s)
-            arrived_w(ZLOW, s)
-
-        @pl.when(step != 0)
-        def _():
-            arrived_w(XALL, s)
-
-        cols = pl.ds(pl.multiple_of(s * CHUNK, 128), CHUNK)
-        acc[...] += jnp.dot(rall[:, cols], w[s], preferred_element_type=jnp.float32)
-        return carry
-
-    lax.fori_loop(0, SLOTS, multiply, 0)
+    acc[ROWS:] = product(ROWS, ROWS, (p + 0) % NH)
+    for plane in ("near", "far"):
+        acc[...] += product(0, 2 * ROWS, whole_plane(plane))
 
     sums = acc[ROWS:]
     amax = jnp.max(jnp.max(jnp.abs(sums), axis=0, keepdims=True), axis=1, keepdims=True)
@@ -243,7 +250,9 @@
     arrived(pin, p_s, p_r)
     arrived(kin, k_s, k_r)
     projected = acc[:ROWS] + pin[...].astype(jnp.int32).astype(jnp.float32) * kin[0:1, 0:1]
-    out[...] = projected.astype(out.dtype)
+    projected_out[...] = projected.astype(out.dtype)
+    result = pltpu.make_async_copy(projected_out, out, out_sem)
+    result.start()
 
     def over_columns(v):
         return jnp.sum((v[:, :128] + v[:, 128:]).T, axis=0, keepdims=True)
@@ -263,6 +272,7 @@
     total = jnp.sum(zs[...], axis=0)
     scores[...] = total[1:2] / jnp.sqrt(total[0:1] / D + 1e-06)
 
+    result.wait()
     for copy in sent:
         copy.wait_send()
 
@@ -274,6 +284,7 @@
 
 def on_device(codes, offsets, responses, head):
     vmem = pl.BlockSpec(memory_space=pltpu.VMEM)
+    hbm = pl.BlockSpec(memory_space=pl.ANY)
     dma = pltpu.SemaphoreType.DMA
     f32, bf16 = jnp.float32, jnp.bfloat16
     out, scores = pl.pallas_call(
@@ -282,9 +293,14 @@
             jax.ShapeDtypeStruct((ROWS, COLS), bf16),
             jax.ShapeDtypeStruct((1, ROWS), f32),
         ),
-        in_specs=[vmem, vmem, pl.BlockSpec(memory_space=pl.ANY), vmem],
-        out_specs=(vmem, vmem),
+        in_specs=[hbm] * 4,
+        out_specs=(hbm, vmem),
         scratch_shapes=[
+            pltpu.VMEM((CHUNK, COLS), bf16),
+            pltpu.VMEM((COLS // BLK, CHUNK // BLK), jnp.int32),
+            pltpu.VMEM((COLS,), bf16),
+            pltpu.VMEM((ROWS, COLS), bf16),
+            dma((3,)), dma,
             pltpu.VMEM((2 * ROWS, HALF), bf16),
             pltpu.VMEM((SLOTS, CHUNK, COLS), bf16),
             pltpu.VMEM((2 * ROWS, COLS), f32),

time: 78.2 us -> 79.7 us (1.019)
  Pallas kernels: 77.4 us -> 78.8 us
    pallas_call x1, Pallas kernels: 75.8 us -> 77.2 us  [on_device(): pl.pallas_call(kernel, out_shape=(jax.ShapeDtypeStruct((ROWS, COLS), bf16...]
where the time goes in v4:
time: 79.7 us; the launch traced here: 79.4 us
  Pallas kernels  78.8 us (99%)
    pallas_call x1, Pallas kernels, on_device(): pl.pallas_call(kernel, out_shape=(jax.ShapeDtypeStruct((ROWS, COLS), bf16...  77.2 us

profile of v4, /device:TPU:1, one launch (start us, length us, event | category | flops | bytes accessed | tf_op | source)
XLA Modules:
  0.0 79.4 jit_solution(18369370071033532454)
XLA Ops:
  0.6 77.2 %project_and_score.1 = (bf16[256,256]{1,0:T(8,128)(2,1)}, f32[1,256]{1,0:T(1,128)}) custom-call(bf16[640,256]{1,0:T(8,128)(2,1)} %codes_in.1, s32[2,5]{1,0:T(2,128)} %bitcast.2, bf16[256,15360]{1,0:T(8,128)(2,1)} %responses.1, bf16[256]{0:T(256)(128)(2,1)} %head_in.1), custom_call_target="tpu_custom_call" | custom-call | flops 2013265920 | bytes 8388608 | tf_op jit(solution)/shard_map/project_and_score/pallas_call | solution.py:290
  77.8 1.6 %results.1 = (bf16[256,256]{1,0:T(8,128)(2,1)}, f32[1,256]{1,0:T(1,128)}) custom-call(bf16[256,256]{1,0:T(8,128)(2,1)} %get-tuple-element.6.out_in, f32[1,256]{1,0:T(1,128)} %get-tuple-element.7.scores_in), custom_call_target="tpu_custom_call" | custom-call | tf_op jit(solution)/shard_map/results/pallas_call | solution.py:328

commit v5 on v4

--- a/solution.py
+++ b/solution.py
@@ -14,7 +14,7 @@
 COLS = 256
 HALF = NX * NH * CHUNK
 SLOTS = NX * NH
-ZF = 496
+ZF = 464
 ZT, XT = (ZF // 2 + 15) // 16 * 16, ((CHUNK - ZF) // 2 + 15) // 16 * 16
 PARTS = ((0, ZF), (0, ZT), (ZT, ZF - ZT), (ZF, CHUNK - ZF), (ZF, XT), (ZF + XT, CHUNK - ZF - XT))
 ZALL, ZTOP, ZLOW, XALL, XTOP, XLOW = range(len(PARTS))
@@ -23,21 +23,21 @@
 PIECE = ROWS // (2 * NY)
 PLANE = NX * CHUNK
 ORDER = (
-    ("rows", 0), ("x", XALL, 1), ("x", ZALL, 1), ("rows", 1),
-    ("z", ZALL, "near"), ("x", ZALL, 3), ("rows", 2), ("rows", 3),
-    ("z", ZALL, "far"), ("start", 0), ("x", XALL, 3), ("start", 1),
-    ("pass", ZALL, "own", 3), ("pass", ZALL, "own", 1), ("ring", -1, 1, 1), ("ring", 1, 0, 1),
-    ("ring", 1, 1, 1), ("ring", -1, 0, 1), ("pass", XALL, "own", 3), ("start", 2),
-    ("turn_x", "near"), ("ring", -1, 0, 2), ("ring", 1, 0, 2), ("turn_z", 3),
-    ("turn_z", 0), ("turn_z", 1), ("ring", 1, 2, 1), ("start", 3),
-    ("ring", -1, 1, 2), ("ring", 1, 2, 2), ("pass", XALL, "own", 1), ("ring", -1, 3, 1),
-    ("ring", 1, 0, 3), ("ring", -1, 2, 1), ("ring", 1, 1, 2), ("turn_x", "far"),
-    ("ring", 1, 3, 1), ("pass", ZALL, "near", 3), ("ring", 1, 2, 3), ("ring", -1, 3, 2),
-    ("ring", -1, 1, 3), ("ring", 1, 0, 4), ("ring", -1, 3, 3), ("ring", -1, 2, 2),
-    ("ring", 1, 3, 2), ("ring", -1, 1, 4), ("pass", ZALL, "near", 1), ("turn_z", 2),
-    ("product",), ("ring", 1, 2, 4), ("ring", -1, 0, 3), ("pass", ZALL, "far", 3),
-    ("pass", ZALL, "far", 1), ("ring", 1, 3, 3), ("ring", -1, 3, 4), ("ring", -1, 2, 3),
-    ("ring", 1, 1, 3),
+    ("rows", 0), ("rows", 3), ("rows", 1), ("z", ZALL, "far"),
+    ("rows", 2), ("x", XALL, 1), ("x", ZALL, 1), ("x", XALL, 3),
+    ("x", ZALL, 3), ("start", 0), ("pass", XALL, "own", 3), ("pass", ZALL, "own", 1),
+    ("z", ZALL, "near"), ("start", 1), ("start", 3), ("pass", XALL, "own", 1),
+    ("ring", -1, 1, 1), ("ring", 1, 0, 1), ("pass", ZALL, "own", 3), ("turn_z", 1),
+    ("ring", -1, 3, 1), ("start", 2), ("word_z",), ("ring", 1, 3, 1),
+    ("ring", -1, 1, 2), ("ring", 1, 1, 1), ("turn_x", "near"), ("ring", -1, 0, 1),
+    ("ring", 1, 0, 2), ("ring", -1, 3, 2), ("ring", 1, 2, 1), ("product",),
+    ("turn_z", 3), ("turn_x", "far"), ("ring", 1, 0, 3), ("ring", -1, 2, 1),
+    ("turn_z", 0), ("word_on",), ("ring", 1, 2, 2), ("pass", ZALL, "near", 1),
+    ("ring", -1, 1, 3), ("turn_z", 2), ("ring", -1, 2, 2), ("ring", -1, 3, 3),
+    ("ring", 1, 3, 2), ("pass", ZALL, "near", 3), ("ring", 1, 1, 2), ("ring", -1, 0, 2),
+    ("ring", -1, 1, 4), ("ring", 1, 2, 3), ("ring", 1, 3, 3), ("ring", 1, 1, 3),
+    ("ring", 1, 0, 4), ("pass", ZALL, "far", 1), ("pass", ZALL, "far", 3), ("ring", -1, 2, 3),
+    ("ring", -1, 0, 3), ("ring", 1, 2, 4), ("ring", -1, 3, 4), ("word_core",),
 )
 
 
@@ -50,7 +50,7 @@
     codes, offsets, head, projected_out, in_sem, out_sem,
     rall, w, acc, pout, pin, kout, kin, ys, zs,
     own_sem, inj_s, inj_r, ring_s, ring_r, sib_s, sib_r,
-    w_s, w_r, p_s, p_r, k_s, k_r, sc_s, sc_r,
+    w_s, w_r, p_s, p_r, k_s, k_r, sc_s, sc_r, word,
 ):
     f, t = lax.axis_index("fsdp"), lax.axis_index("tp")
     x, zl = f % NX, f // NX
@@ -77,9 +77,7 @@
     rest = [device(x, y, zl, (zh + g) % 2, (c + k) % 2) for g, k in ((0, 1), (1, 0), (1, 1))]
 
     barrier = pltpu.get_barrier_semaphore()
-    partners = [mate, *wants, *rest, at_x(1), at_x(3)]
-    partners += [at_z(e) for e in range(1, NH)]
-    partners += [at_y(e) for e in range(1, NY)]
+    partners = [sibling, *wants, at_x(1), at_x(3), at_z(1), at_z(2), at_y(1), at_y(-1)]
     for partner in partners:
         pl.semaphore_signal(barrier, inc=1, device_id=partner, device_id_type=MESH)
 
@@ -110,6 +108,13 @@
             w[mine, i * BLK : (i + 1) * BLK, j * BLK : (j + 1) * BLK] = (block * scale).astype(jnp.bfloat16)
 
     pl.semaphore_wait(barrier, len(partners))
+
+    def tell(n, *to):
+        for one in to:
+            pl.semaphore_signal(word.at[n], inc=1, device_id=one, device_id_type=MESH)
+
+    def hear(n, number):
+        pl.semaphore_wait(word.at[n], number)
 
     sent = []
 
@@ -227,18 +232,31 @@
         own.wait()
         acc[:ROWS] = product(0, ROWS, whole_plane("own"))
 
+    def word_z():
+        tell(0, at_z(1), at_z(2))
+
+    def word_on():
+        hear(0, 2)
+        tell(1, *wants)
+
+    def word_core():
+        hear(1, 2)
+        tell(2, sibling)
+
     steps_of = {
         "rows": send_rows, "start": ring_start, "ring": ring, "x": start_x, "z": start_z,
         "pass": pass_x, "turn_z": turn_z, "turn_x": turn_x, "product": own_rows,
+        "word_z": word_z, "word_on": word_on, "word_core": word_core,
     }
     for name, *what in ORDER:
         steps_of[name](*what)
 
+    hear(2, 1)
     for yo, k, n in sibs:
         arrived(piece(yo, 1 - c, k), sib_s.at[n], sib_r.at[n])
-    acc[ROWS:] = product(ROWS, ROWS, (p + 0) % NH)
+    acc[ROWS:] = product(ROWS, ROWS, p)
     for plane in ("near", "far"):
-        acc[...] += product(0, 2 * ROWS, whole_plane(plane))
+        acc[ROWS:] += product(ROWS, ROWS, whole_plane(plane))
 
     sums = acc[ROWS:]
     amax = jnp.max(jnp.max(jnp.abs(sums), axis=0, keepdims=True), axis=1, keepdims=True)
@@ -247,6 +265,8 @@
     kout[...] = jnp.broadcast_to(unit, kout.shape)
     send(pout, pin, p_s, p_r, mate)
     send(kout, kin, k_s, k_r, mate)
+    for plane in ("near", "far"):
+        acc[:ROWS] += product(0, ROWS, (p + planes[plane]) % NH)
     arrived(pin, p_s, p_r)
     arrived(kin, k_s, k_r)
     projected = acc[:ROWS] + pin[...].astype(jnp.int32).astype(jnp.float32) * kin[0:1, 0:1]
@@ -318,6 +338,7 @@
             dma, dma,
             dma, dma,
             dma((NY + 3,)), dma((NY + 3,)),
+            pltpu.SemaphoreType.REGULAR((3,)),
         ],
         compiler_params=pltpu.CompilerParams(
             collective_id=0, has_side_effects=True, vmem_limit_bytes=60 * 2**20

time: 79.7 us -> 78.5 us (0.985)
  Pallas kernels: 78.8 us -> 77.7 us
    pallas_call x1, Pallas kernels: 77.2 us -> 76.2 us  [on_device(): pl.pallas_call(kernel, out_shape=(jax.ShapeDtypeStruct((ROWS, COLS), bf16...]
where the time goes in v5:
time: 78.5 us; the launch traced here: 78.4 us
  Pallas kernels  77.7 us (99%)
    pallas_call x1, Pallas kernels, on_device(): pl.pallas_call(kernel, out_shape=(jax.ShapeDtypeStruct((ROWS, COLS), bf16...  76.2 us
    pallas_call x1, Pallas kernels, on_device(): pl.pallas_call(results, out_shape=(jax.ShapeDtypeStruct((ROWS, COLS), bf1...  1.57 us

profile of v5, /device:TPU:1, one launch (start us, length us, event | category | flops | bytes accessed | tf_op | source)
XLA Modules:
  0.0 78.4 jit_solution(18220834256533828084)
XLA Ops:
  0.6 76.2 %project_and_score.1 = (bf16[256,256]{1,0:T(8,128)(2,1)}, f32[1,256]{1,0:T(1,128)}) custom-call(bf16[640,256]{1,0:T(8,128)(2,1)} %codes_in.1, s32[2,5]{1,0:T(2,128)} %bitcast.2, bf16[256,15360]{1,0:T(8,128)(2,1)} %responses.1, bf16[256]{0:T(256)(128)(2,1)} %head_in.1), custom_call_target="tpu_custom_call" | custom-call | flops 2013265920 | bytes 8388608 | tf_op jit(solution)/shard_map/project_and_score/pallas_call | solution.py:310
  76.8 1.6 %results.1 = (bf16[256,256]{1,0:T(8,128)(2,1)}, f32[1,256]{1,0:T(1,128)}) custom-call(bf16[256,256]{1,0:T(8,128)(2,1)} %get-tuple-element.6.out_in, f32[1,256]{1,0:T(1,128)} %get-tuple-element.7.scores_in), custom_call_target="tpu_custom_call" | custom-call | tf_op jit(solution)/shard_map/results/pallas_call | solution.py:349

commit v6 on v5

--- a/solution.py
+++ b/solution.py
@@ -12,9 +12,10 @@
 ROWS = 256
 CHUNK = 640
 COLS = 256
+NHALF = 128
 HALF = NX * NH * CHUNK
 SLOTS = NX * NH
-ZF = 464
+ZF = 480
 ZT, XT = (ZF // 2 + 15) // 16 * 16, ((CHUNK - ZF) // 2 + 15) // 16 * 16
 PARTS = ((0, ZF), (0, ZT), (ZT, ZF - ZT), (ZF, CHUNK - ZF), (ZF, XT), (ZF + XT, CHUNK - ZF - XT))
 ZALL, ZTOP, ZLOW, XALL, XTOP, XLOW = range(len(PARTS))
@@ -23,21 +24,27 @@
 PIECE = ROWS // (2 * NY)
 PLANE = NX * CHUNK
 ORDER = (
-    ("rows", 0), ("rows", 3), ("rows", 1), ("z", ZALL, "far"),
-    ("rows", 2), ("x", XALL, 1), ("x", ZALL, 1), ("x", XALL, 3),
-    ("x", ZALL, 3), ("start", 0), ("pass", XALL, "own", 3), ("pass", ZALL, "own", 1),
-    ("z", ZALL, "near"), ("start", 1), ("start", 3), ("pass", XALL, "own", 1),
-    ("ring", -1, 1, 1), ("ring", 1, 0, 1), ("pass", ZALL, "own", 3), ("turn_z", 1),
-    ("ring", -1, 3, 1), ("start", 2), ("word_z",), ("ring", 1, 3, 1),
-    ("ring", -1, 1, 2), ("ring", 1, 1, 1), ("turn_x", "near"), ("ring", -1, 0, 1),
-    ("ring", 1, 0, 2), ("ring", -1, 3, 2), ("ring", 1, 2, 1), ("product",),
-    ("turn_z", 3), ("turn_x", "far"), ("ring", 1, 0, 3), ("ring", -1, 2, 1),
-    ("turn_z", 0), ("word_on",), ("ring", 1, 2, 2), ("pass", ZALL, "near", 1),
-    ("ring", -1, 1, 3), ("turn_z", 2), ("ring", -1, 2, 2), ("ring", -1, 3, 3),
-    ("ring", 1, 3, 2), ("pass", ZALL, "near", 3), ("ring", 1, 1, 2), ("ring", -1, 0, 2),
-    ("ring", -1, 1, 4), ("ring", 1, 2, 3), ("ring", 1, 3, 3), ("ring", 1, 1, 3),
-    ("ring", 1, 0, 4), ("pass", ZALL, "far", 1), ("pass", ZALL, "far", 3), ("ring", -1, 2, 3),
-    ("ring", -1, 0, 3), ("ring", 1, 2, 4), ("ring", -1, 3, 4), ("word_core",),
+    ("z", 0, ZALL, "near"), ("z", 0, ZALL, "far"), ("x", 0, XALL, 1), ("rows", 0),
+    ("x", 1, XALL, 3), ("rows", 1), ("x", 1, ZALL, 3), ("rows", 3),
+    ("x", 1, ZALL, 1), ("turn_x", 0, "near"), ("rows", 2), ("start", 1),
+    ("x", 0, XALL, 3), ("start", 0), ("x", 0, ZALL, 1), ("start", 3),
+    ("pass", 0, ZALL, "near", 1), ("ring", 1, 0, 1), ("z", 1, ZALL, "far"), ("ring", -1, 0, 1),
+    ("z", 1, ZALL, "near"), ("start", 2), ("word_z",), ("pass", 0, XALL, "own", 3),
+    ("turn_z", 1, 0), ("turn_z", 0, 3), ("x", 1, XALL, 1), ("pass", 0, XALL, "own", 1),
+    ("ring", -1, 1, 1), ("pass", 1, XALL, "own", 1), ("ring", 1, 3, 1), ("turn_z", 1, 1),
+    ("pass", 0, ZALL, "near", 3), ("ring", 1, 1, 1), ("ring", -1, 3, 1), ("turn_z", 0, 2),
+    ("x", 0, ZALL, 3), ("ring", 1, 2, 1), ("turn_x", 0, "far"), ("ring", 1, 0, 2),
+    ("turn_x", 1, "far"), ("ring", -1, 0, 2), ("ring", -1, 3, 2), ("ring", 1, 3, 2),
+    ("turn_x", 1, "near"), ("turn_z", 0, 1), ("ring", -1, 1, 2), ("ring", 1, 1, 2),
+    ("ring", 1, 2, 2), ("ring", -1, 2, 1), ("pass", 0, ZALL, "own", 1), ("word_on",),
+    ("ring", -1, 3, 3), ("pass", 1, XALL, "own", 3), ("ring", -1, 1, 3), ("pass", 0, ZALL, "far", 3),
+    ("ring", -1, 0, 3), ("pass", 1, ZALL, "far", 3), ("turn_z", 0, 0), ("ring", 1, 0, 3),
+    ("ring", -1, 2, 2), ("ring", 1, 3, 3), ("ring", 1, 2, 3), ("turn_z", 1, 3),
+    ("pass", 0, ZALL, "far", 1), ("pass", 0, ZALL, "own", 3), ("turn_z", 1, 2), ("ring", -1, 1, 4),
+    ("pass", 1, ZALL, "near", 3), ("ring", 1, 0, 4), ("pass", 1, ZALL, "own", 3), ("ring", 1, 1, 3),
+    ("pass", 1, ZALL, "near", 1), ("pass", 1, ZALL, "own", 1), ("pass", 1, ZALL, "far", 1), ("ring", 1, 2, 4),
+    ("ring", -1, 2, 3), ("ring", -1, 3, 4), ("word_core",), ("partial", 0),
+    ("partial", 1),
 )
 
 
@@ -105,7 +112,7 @@
             block = codes[i * BLK : (i + 1) * BLK, j * BLK : (j + 1) * BLK].astype(jnp.float32)
             amax = jnp.max(jnp.max(jnp.abs(block), axis=0, keepdims=True), axis=1, keepdims=True)
             scale = jnp.exp2(offsets[j : j + 1, i : i + 1].astype(jnp.float32)) / (amax + 1e-06)
-            w[mine, i * BLK : (i + 1) * BLK, j * BLK : (j + 1) * BLK] = (block * scale).astype(jnp.bfloat16)
+            w[j, mine, i * BLK : (i + 1) * BLK] = (block * scale).astype(jnp.bfloat16)
 
     pl.semaphore_wait(barrier, len(partners))
 
@@ -136,24 +143,24 @@
         row = pl.multiple_of(ROWS + 2 * PIECE * yo + PIECE * core, PIECE)
         return rall.at[pl.ds(row, PIECE), pl.ds(k * SUB, SUB)]
 
-    def part(kind, s):
+    def part(n, kind, s):
         row, rows = PARTS[kind]
-        return w.at[s, pl.ds(row, rows)]
+        return w.at[n, s, pl.ds(row, rows)]
 
     count = {"w": 0, "ring": 0}
 
-    def send_w(kind, s, to):
-        n = count["w"]
+    def send_w(n, kind, s, to):
+        i = count["w"]
         count["w"] += 1
-        send(part(kind, s), part(kind, s), w_s.at[n], w_r.at[kind, s], to)
+        send(part(n, kind, s), part(n, kind, s), w_s.at[i], w_r.at[n, kind, s], to)
 
     met = set()
 
-    def arrived_w(kind, xe, plane):
-        if (kind, xe, plane) not in met:
-            met.add((kind, xe, plane))
+    def arrived_w(n, kind, xe, plane):
+        if (n, kind, xe, plane) not in met:
+            met.add((n, kind, xe, plane))
             s = slot(xe, planes[plane])
-            arrived(part(kind, s), w_s.at[0], w_r.at[kind, s])
+            arrived(part(n, kind, s), w_s.at[0], w_r.at[n, kind, s])
 
     def send_rows(k):
         row = pl.multiple_of(2 * PIECE * y + PIECE * c, PIECE)
@@ -191,46 +198,57 @@
         ring(1, k, 0)
         ring(-1, k, 0)
 
-    def start_x(kind, to):
-        send_w(kind, mine, at_x(to))
-
-    def start_z(kind, plane):
-        send_w(kind, mine, at_z(planes[plane]))
-
-    def pass_x(kind, plane, xe):
-        arrived_w(kind, xe, plane)
+    def start_x(n, kind, to):
+        send_w(n, kind, mine, at_x(to))
+
+    def start_z(n, kind, plane):
+        send_w(n, kind, mine, at_z(planes[plane]))
+
+    def pass_x(n, kind, plane, xe):
+        arrived_w(n, kind, xe, plane)
         half = {(XALL, 1): XLOW, (XALL, 3): XTOP, (ZALL, 1): ZLOW, (ZALL, 3): ZTOP}[kind, xe]
-        send_w(half, slot(xe, planes[plane]), at_x(NX - xe))
-
-    def turn_z(xe):
+        send_w(n, half, slot(xe, planes[plane]), at_x(NX - xe))
+
+    def turn_z(n, xe):
         if xe:
             for kind in (XTOP, XLOW) if xe == 2 else (XALL,):
-                arrived_w(kind, xe, "own")
+                arrived_w(n, kind, xe, "own")
         for plane in ("near", "far"):
-            send_w(XALL, slot(xe, 0), at_z(planes[plane]))
-
-    def turn_x(plane):
-        arrived_w(ZALL, 0, plane)
+            send_w(n, XALL, slot(xe, 0), at_z(planes[plane]))
+
+    def turn_x(n, plane):
+        arrived_w(n, ZALL, 0, plane)
         for to in (1, 3):
-            send_w(ZALL, slot(0, planes[plane]), at_x(to))
-
-    def whole_plane(plane):
+            send_w(n, ZALL, slot(0, planes[plane]), at_x(to))
+
+    def whole_plane(n, plane):
         for xe in range(NX):
             if xe or plane != "own":
                 for kind in (ZTOP, ZLOW) if xe == 2 else (ZALL,):
-                    arrived_w(kind, xe, plane)
+                    arrived_w(n, kind, xe, plane)
                 for kind in (XTOP, XLOW) if xe == 2 and plane == "own" else (XALL,):
-                    arrived_w(kind, xe, plane)
-        return (p + planes[plane]) % NH
-
-    def product(first, rows, q):
+                    arrived_w(n, kind, xe, plane)
+
+    def product(n, first, q):
         cols = pl.ds(pl.multiple_of(q * PLANE, 128), PLANE)
-        weights = w[pl.ds(q * NX, NX)].reshape(PLANE, COLS)
-        return jnp.dot(rall[pl.ds(first, rows), cols], weights, preferred_element_type=jnp.float32)
-
-    def own_rows():
-        own.wait()
-        acc[:ROWS] = product(0, ROWS, whole_plane("own"))
+        weights = w[n, pl.ds(q * NX, NX)].reshape(PLANE, NHALF)
+        return jnp.dot(rall[pl.ds(first, ROWS), cols], weights, preferred_element_type=jnp.float32)
+
+    def partial(n):
+        if n == 0:
+            for yo, k, i in sibs:
+                arrived(piece(yo, 1 - c, k), sib_s.at[i], sib_r.at[i])
+        whole_plane(n, "own")
+        sums = product(n, ROWS, p)
+        for plane in ("near", "far"):
+            whole_plane(n, plane)
+            sums += product(n, ROWS, (p + planes[plane]) % NH)
+        amax = jnp.max(jnp.max(jnp.abs(sums), axis=0, keepdims=True), axis=1, keepdims=True)
+        unit = jnp.maximum(amax, 1e-30) / 32760.0
+        pout[n] = jnp.floor(sums * (1.0 / unit) + 0.5).astype(jnp.int32).astype(jnp.int16)
+        kout[n] = jnp.broadcast_to(unit, kout.shape[1:])
+        send(pout.at[n], pin.at[n], p_s.at[n], p_r.at[n], mate)
+        send(kout.at[n], kin.at[n], k_s.at[n], k_r.at[n], mate)
 
     def word_z():
         tell(0, at_z(1), at_z(2))
@@ -245,40 +263,37 @@
 
     steps_of = {
         "rows": send_rows, "start": ring_start, "ring": ring, "x": start_x, "z": start_z,
-        "pass": pass_x, "turn_z": turn_z, "turn_x": turn_x, "product": own_rows,
+        "pass": pass_x, "turn_z": turn_z, "turn_x": turn_x, "partial": partial,
         "word_z": word_z, "word_on": word_on, "word_core": word_core,
     }
     for name, *what in ORDER:
         steps_of[name](*what)
 
     hear(2, 1)
-    for yo, k, n in sibs:
-        arrived(piece(yo, 1 - c, k), sib_s.at[n], sib_r.at[n])
-    acc[ROWS:] = product(ROWS, ROWS, p)
-    for plane in ("near", "far"):
-        acc[ROWS:] += product(ROWS, ROWS, whole_plane(plane))
-
-    sums = acc[ROWS:]
-    amax = jnp.max(jnp.max(jnp.abs(sums), axis=0, keepdims=True), axis=1, keepdims=True)
-    unit = jnp.maximum(amax, 1e-30) / 32760.0
-    pout[...] = jnp.floor(sums * (1.0 / unit) + 0.5).astype(jnp.int32).astype(jnp.int16)
-    kout[...] = jnp.broadcast_to(unit, kout.shape)
-    send(pout, pin, p_s, p_r, mate)
-    send(kout, kin, k_s, k_r, mate)
-    for plane in ("near", "far"):
-        acc[:ROWS] += product(0, ROWS, (p + planes[plane]) % NH)
-    arrived(pin, p_s, p_r)
-    arrived(kin, k_s, k_r)
-    projected = acc[:ROWS] + pin[...].astype(jnp.int32).astype(jnp.float32) * kin[0:1, 0:1]
-    projected_out[...] = projected.astype(out.dtype)
+    own.wait()
+    acc[...] = jnp.zeros_like(acc)
+
+    def own_rows(i, carry):
+        acc[i // NH] += product(i // NH, 0, i % NH)
+        return carry
+
+    lax.fori_loop(0, 2 * NH, own_rows, 0)
+    halves = []
+    for n in range(2):
+        arrived(pin.at[n], p_s.at[n], p_r.at[n])
+        arrived(kin.at[n], k_s.at[n], k_r.at[n])
+        halves.append(acc[n] + pin[n].astype(jnp.int32).astype(jnp.float32) * kin[n, 0:1, 0:1])
+        projected_out[:, n * NHALF : (n + 1) * NHALF] = halves[n].astype(out.dtype)
     result = pltpu.make_async_copy(projected_out, out, out_sem)
     result.start()
 
     def over_columns(v):
-        return jnp.sum((v[:, :128] + v[:, 128:]).T, axis=0, keepdims=True)
-
-    ys[y, 0:1] = over_columns(projected * projected)
-    ys[y, 1:2] = over_columns(projected * head[...].astype(jnp.float32).reshape(1, COLS))
+        return jnp.sum(v.T, axis=0, keepdims=True)
+
+    heads = head[...].astype(jnp.float32).reshape(1, COLS)
+    first, second = halves
+    ys[y, 0:1] = over_columns(first * first + second * second)
+    ys[y, 1:2] = over_columns(first * heads[:, :NHALF] + second * heads[:, NHALF:])
     for e in range(1, NY):
         send(ys.at[y], ys.at[y], sc_s.at[e], sc_r.at[e], at_y(e))
     for e in range(1, NY):
@@ -322,21 +337,21 @@
             pltpu.VMEM((ROWS, COLS), bf16),
             dma((3,)), dma,
             pltpu.VMEM((2 * ROWS, HALF), bf16),
-            pltpu.VMEM((SLOTS, CHUNK, COLS), bf16),
-            pltpu.VMEM((2 * ROWS, COLS), f32),
-            pltpu.VMEM((ROWS, COLS), jnp.int16),
-            pltpu.VMEM((ROWS, COLS), jnp.int16),
-            pltpu.VMEM((8, 128), f32),
-            pltpu.VMEM((8, 128), f32),
+            pltpu.VMEM((2, SLOTS, CHUNK, NHALF), bf16),
+            pltpu.VMEM((2, ROWS, NHALF), f32),
+            pltpu.VMEM((2, ROWS, NHALF), jnp.int16),
+            pltpu.VMEM((2, ROWS, NHALF), jnp.int16),
+            pltpu.VMEM((2, 8, 128), f32),
+            pltpu.VMEM((2, 8, 128), f32),
             pltpu.VMEM((NY, 2, ROWS), f32),
             pltpu.VMEM((4, 2, ROWS), f32),
             dma,
             dma((SUBS,)), dma((SUBS,)),
             dma((8 * SUBS,)), dma((8 * SUBS,)),
             dma((8 * SUBS,)), dma((8 * SUBS,)),
-            dma((2 * SLOTS + 4,)), dma((len(PARTS), SLOTS)),
-            dma, dma,
-            dma, dma,
+            dma((4 * SLOTS + 8,)), dma((2, len(PARTS), SLOTS)),
+            dma((2,)), dma((2,)),
+            dma((2,)), dma((2,)),
             dma((NY + 3,)), dma((NY + 3,)),
             pltpu.SemaphoreType.REGULAR((3,)),
         ],

time: 78.5 us -> 76.1 us (0.969)
  Pallas kernels: 77.7 us -> 75.3 us
    pallas_call x1, Pallas kernels: 76.2 us -> 73.7 us  [on_device(): pl.pallas_call(kernel, out_shape=(jax.ShapeDtypeStruct((ROWS, COLS), bf16...]
where the time goes in v6:
time: 76.1 us; the launch traced here: 75.9 us
  Pallas kernels  75.3 us (99%)
    pallas_call x1, Pallas kernels, on_device(): pl.pallas_call(kernel, out_shape=(jax.ShapeDtypeStruct((ROWS, COLS), bf16...  73.7 us
    pallas_call x1, Pallas kernels, on_device(): pl.pallas_call(results, out_shape=(jax.ShapeDtypeStruct((ROWS, COLS), bf1...  1.57 us

profile of v6, /device:TPU:1, one launch (start us, length us, event | category | flops | bytes accessed | tf_op | source)
XLA Modules:
  0.0 75.9 jit_solution(10564119076243312216)
XLA Ops:
  0.6 73.7 %project_and_score.1 = (bf16[256,256]{1,0:T(8,128)(2,1)}, f32[1,256]{1,0:T(1,128)}) custom-call(bf16[640,256]{1,0:T(8,128)(2,1)} %codes_in.1, s32[2,5]{1,0:T(2,128)} %bitcast.2, bf16[256,15360]{1,0:T(8,128)(2,1)} %responses.1, bf16[256]{0:T(256)(128)(2,1)} %head_in.1), custom_call_target="tpu_custom_call" | custom-call | flops 2013265920 | bytes 8388608 | tf_op jit(solution)/shard_map/project_and_score/pallas_call | solution.py:325
  74.4 1.6 %results.1 = (bf16[256,256]{1,0:T(8,128)(2,1)}, f32[1,256]{1,0:T(1,128)}) custom-call(bf16[256,256]{1,0:T(8,128)(2,1)} %get-tuple-element.6.out_in, f32[1,256]{1,0:T(1,128)} %get-tuple-element.7.scores_in), custom_call_target="tpu_custom_call" | custom-call | tf_op jit(solution)/shard_map/results/pallas_call | solution.py:364

commit v7 on v6

--- a/solution.py
+++ b/solution.py
@@ -278,6 +278,9 @@
         return carry
 
     lax.fori_loop(0, 2 * NH, own_rows, 0)
+    for copy in sent[:-4]:
+        copy.wait_send()
+    del sent[:-4]
     halves = []
     for n in range(2):
         arrived(pin.at[n], p_s.at[n], p_r.at[n])

time: 76.1 us -> 75.9 us (level)
  no operation moved by 1% of the time
where the time goes in v7:
time: 75.9 us; the launch traced here: 75.8 us
  Pallas kernels  75.1 us (99%)
    pallas_call x1, Pallas kernels, on_device(): pl.pallas_call(kernel, out_shape=(jax.ShapeDtypeStruct((ROWS, COLS), bf16...  73.5 us
    pallas_call x1, Pallas kernels, on_device(): pl.pallas_call(results, out_shape=(jax.ShapeDtypeStruct((ROWS, COLS), bf1...  1.57 us

profile of v7, /device:TPU:1, one launch (start us, length us, event | category | flops | bytes accessed | tf_op | source)
XLA Modules:
  0.0 75.8 jit_solution(9246621445002544693)
XLA Ops:
  0.6 73.5 %project_and_score.1 = (bf16[256,256]{1,0:T(8,128)(2,1)}, f32[1,256]{1,0:T(1,128)}) custom-call(bf16[640,256]{1,0:T(8,128)(2,1)} %codes_in.1, s32[2,5]{1,0:T(2,128)} %bitcast.2, bf16[256,15360]{1,0:T(8,128)(2,1)} %responses.1, bf16[256]{0:T(256)(128)(2,1)} %head_in.1), custom_call_target="tpu_custom_call" | custom-call | flops 2013265920 | bytes 8388608 | tf_op jit(solution)/shard_map/project_and_score/pallas_call | solution.py:328
  74.2 1.6 %results.1 = (bf16[256,256]{1,0:T(8,128)(2,1)}, f32[1,256]{1,0:T(1,128)}) custom-call(bf16[256,256]{1,0:T(8,128)(2,1)} %get-tuple-element.6.out_in, f32[1,256]{1,0:T(1,128)} %get-tuple-element.7.scores_in), custom_call_target="tpu_custom_call" | custom-call | tf_op jit(solution)/shard_map/results/pallas_call | solution.py:367

commit v8 on v7

--- a/solution.py
+++ b/solution.py
@@ -15,7 +15,7 @@
 NHALF = 128
 HALF = NX * NH * CHUNK
 SLOTS = NX * NH
-ZF = 480
+ZF = 512
 ZT, XT = (ZF // 2 + 15) // 16 * 16, ((CHUNK - ZF) // 2 + 15) // 16 * 16
 PARTS = ((0, ZF), (0, ZT), (ZT, ZF - ZT), (ZF, CHUNK - ZF), (ZF, XT), (ZF + XT, CHUNK - ZF - XT))
 ZALL, ZTOP, ZLOW, XALL, XTOP, XLOW = range(len(PARTS))
@@ -24,26 +24,26 @@
 PIECE = ROWS // (2 * NY)
 PLANE = NX * CHUNK
 ORDER = (
-    ("z", 0, ZALL, "near"), ("z", 0, ZALL, "far"), ("x", 0, XALL, 1), ("rows", 0),
-    ("x", 1, XALL, 3), ("rows", 1), ("x", 1, ZALL, 3), ("rows", 3),
-    ("x", 1, ZALL, 1), ("turn_x", 0, "near"), ("rows", 2), ("start", 1),
-    ("x", 0, XALL, 3), ("start", 0), ("x", 0, ZALL, 1), ("start", 3),
-    ("pass", 0, ZALL, "near", 1), ("ring", 1, 0, 1), ("z", 1, ZALL, "far"), ("ring", -1, 0, 1),
-    ("z", 1, ZALL, "near"), ("start", 2), ("word_z",), ("pass", 0, XALL, "own", 3),
-    ("turn_z", 1, 0), ("turn_z", 0, 3), ("x", 1, XALL, 1), ("pass", 0, XALL, "own", 1),
-    ("ring", -1, 1, 1), ("pass", 1, XALL, "own", 1), ("ring", 1, 3, 1), ("turn_z", 1, 1),
-    ("pass", 0, ZALL, "near", 3), ("ring", 1, 1, 1), ("ring", -1, 3, 1), ("turn_z", 0, 2),
-    ("x", 0, ZALL, 3), ("ring", 1, 2, 1), ("turn_x", 0, "far"), ("ring", 1, 0, 2),
-    ("turn_x", 1, "far"), ("ring", -1, 0, 2), ("ring", -1, 3, 2), ("ring", 1, 3, 2),
-    ("turn_x", 1, "near"), ("turn_z", 0, 1), ("ring", -1, 1, 2), ("ring", 1, 1, 2),
-    ("ring", 1, 2, 2), ("ring", -1, 2, 1), ("pass", 0, ZALL, "own", 1), ("word_on",),
-    ("ring", -1, 3, 3), ("pass", 1, XALL, "own", 3), ("ring", -1, 1, 3), ("pass", 0, ZALL, "far", 3),
-    ("ring", -1, 0, 3), ("pass", 1, ZALL, "far", 3), ("turn_z", 0, 0), ("ring", 1, 0, 3),
-    ("ring", -1, 2, 2), ("ring", 1, 3, 3), ("ring", 1, 2, 3), ("turn_z", 1, 3),
-    ("pass", 0, ZALL, "far", 1), ("pass", 0, ZALL, "own", 3), ("turn_z", 1, 2), ("ring", -1, 1, 4),
-    ("pass", 1, ZALL, "near", 3), ("ring", 1, 0, 4), ("pass", 1, ZALL, "own", 3), ("ring", 1, 1, 3),
-    ("pass", 1, ZALL, "near", 1), ("pass", 1, ZALL, "own", 1), ("pass", 1, ZALL, "far", 1), ("ring", 1, 2, 4),
-    ("ring", -1, 2, 3), ("ring", -1, 3, 4), ("word_core",), ("partial", 0),
+    ("z", 0, ZALL, "near"), ("rows", 3), ("x", 1, ZALL, 1), ("rows", 0),
+    ("rows", 2), ("x", 0, ZALL, 3), ("x", 0, XALL, 3), ("x", 1, XALL, 3),
+    ("x", 1, XALL, 1), ("start", 3), ("x", 0, ZALL, 1), ("x", 1, ZALL, 3),
+    ("rows", 1), ("z", 0, ZALL, "far"), ("start", 0), ("pass", 1, ZALL, "own", 3),
+    ("pass", 0, XALL, "own", 1), ("x", 0, XALL, 1), ("start", 2), ("ring", 1, 0, 1),
+    ("ring", -1, 0, 1), ("ring", 1, 3, 1), ("z", 1, ZALL, "far"), ("pass", 0, ZALL, "own", 3),
+    ("z", 1, ZALL, "near"), ("ring", -1, 3, 1), ("pass", 0, ZALL, "own", 1), ("turn_x", 0, "near"),
+    ("turn_z", 0, 1), ("pass", 0, XALL, "own", 3), ("pass", 1, XALL, "own", 1), ("ring", 1, 0, 2),
+    ("ring", -1, 0, 2), ("turn_z", 0, 0), ("start", 1), ("word_z",),
+    ("ring", 1, 3, 2), ("turn_x", 0, "far"), ("ring", -1, 3, 2), ("ring", 1, 2, 1),
+    ("ring", -1, 2, 1), ("turn_z", 0, 3), ("ring", 1, 1, 1), ("ring", -1, 1, 1),
+    ("turn_x", 1, "near"), ("pass", 0, ZALL, "near", 1), ("turn_z", 0, 2), ("ring", 1, 2, 2),
+    ("ring", -1, 2, 2), ("pass", 1, XALL, "own", 3), ("ring", 1, 1, 2), ("ring", -1, 1, 2),
+    ("turn_z", 1, 0), ("ring", 1, 0, 3), ("pass", 0, ZALL, "far", 1), ("ring", -1, 3, 3),
+    ("turn_x", 1, "far"), ("word_on",), ("ring", 1, 2, 3), ("turn_z", 1, 1),
+    ("pass", 0, ZALL, "near", 3), ("ring", -1, 0, 3), ("pass", 1, ZALL, "own", 1), ("ring", -1, 1, 3),
+    ("turn_z", 1, 3), ("ring", 1, 0, 4), ("ring", -1, 2, 3), ("pass", 1, ZALL, "near", 1),
+    ("ring", -1, 3, 4), ("pass", 0, ZALL, "far", 3), ("ring", 1, 1, 3), ("pass", 1, ZALL, "near", 3),
+    ("turn_z", 1, 2), ("ring", -1, 1, 4), ("ring", 1, 2, 4), ("pass", 1, ZALL, "far", 3),
+    ("ring", 1, 3, 3), ("word_core",), ("partial", 0), ("pass", 1, ZALL, "far", 1),
     ("partial", 1),
 )
 
@@ -75,16 +75,14 @@
     def at_y(e):
         return device(x, (y + e + NY) % NY, zl, zh, c)
 
-    mate = device(x, y, NZ - 1 - zl, zh, c)
-    outer, middle = (zl == 0) | (zl == NZ - 1), (zl == NH - 1) | (zl == NH)
-    wants = [
-        device(x, y, NZ - 1 - zl, jnp.where(outer, 1 - zh, zh), c),
-        device(x, y, NZ - 1 - zl, jnp.where(middle, zh, 1 - zh), c),
-    ]
+    middle = (zl == NH - 1) | (zl == NH)
+    mate_zl = jnp.where(middle, NZ - 1 - zl, (zl + 4) % 8)
+    mate = device(x, y, mate_zl, zh, c)
+    wants = device(x, y, mate_zl, jnp.where(middle, zh, 1 - zh), c)
     rest = [device(x, y, zl, (zh + g) % 2, (c + k) % 2) for g, k in ((0, 1), (1, 0), (1, 1))]
 
     barrier = pltpu.get_barrier_semaphore()
-    partners = [sibling, *wants, at_x(1), at_x(3), at_z(1), at_z(2), at_y(1), at_y(-1)]
+    partners = [sibling, wants, at_x(1), at_x(3), at_z(1), at_z(2), at_y(1), at_y(-1)]
     for partner in partners:
         pl.semaphore_signal(barrier, inc=1, device_id=partner, device_id_type=MESH)
 
@@ -167,7 +165,7 @@
         col = pl.multiple_of((1 - h) * HALF + k * SUB, 128)
         send(
             responses.at[pl.ds(row, PIECE), pl.ds(col, SUB)],
-            piece(y, c, k), inj_s.at[k], inj_r.at[k], wants[k % 2],
+            piece(y, c, k), inj_s.at[k], inj_r.at[k], wants,
         )
 
     near = jnp.where(p == NH - 1, 2, 1)
@@ -255,10 +253,10 @@
 
     def word_on():
         hear(0, 2)
-        tell(1, *wants)
+        tell(1, wants)
 
     def word_core():
-        hear(1, 2)
+        hear(1, 1)
         tell(2, sibling)
 
     steps_of = {

time: 75.9 us -> 80.4 us (1.059)
  Pallas kernels: 75.1 us -> 79.6 us
    pallas_call x1, Pallas kernels: 73.5 us -> 78.1 us  [on_device(): pl.pallas_call(kernel, out_shape=(jax.ShapeDtypeStruct((ROWS, COLS), bf16...]
where the time goes in v8:
time: 80.4 us; the launch traced here: 80.3 us
  Pallas kernels  79.6 us (99%)
    pallas_call x1, Pallas kernels, on_device(): pl.pallas_call(kernel, out_shape=(jax.ShapeDtypeStruct((ROWS, COLS), bf16...  78.1 us

profile of v8, /device:TPU:1, one launch (start us, length us, event | category | flops | bytes accessed | tf_op | source)
XLA Modules:
  0.0 80.3 jit_solution(13058563184312227905)
XLA Ops:
  0.6 78.1 %project_and_score.1 = (bf16[256,256]{1,0:T(8,128)(2,1)}, f32[1,256]{1,0:T(1,128)}) custom-call(bf16[640,256]{1,0:T(8,128)(2,1)} %codes_in.1, s32[2,5]{1,0:T(2,128)} %bitcast.2, bf16[256,15360]{1,0:T(8,128)(2,1)} %responses.1, bf16[256]{0:T(256)(128)(2,1)} %head_in.1), custom_call_target="tpu_custom_call" | custom-call | flops 2013265920 | bytes 8388608 | tf_op jit(solution)/shard_map/project_and_score/pallas_call | solution.py:326
  78.7 1.6 %results.1 = (bf16[256,256]{1,0:T(8,128)(2,1)}, f32[1,256]{1,0:T(1,128)}) custom-call(bf16[256,256]{1,0:T(8,128)(2,1)} %get-tuple-element.6.out_in, f32[1,256]{1,0:T(1,128)} %get-tuple-element.7.scores_in), custom_call_target="tpu_custom_call" | custom-call | tf_op jit(solution)/shard_map/results/pallas_call | solution.py:365
